TPU v7x, 128 devices: a whole 4x4x4 slice. The times are simulated.
128 devices in a mesh: tm: 8 (over x, y_lo), space: 16 (over z, y_hi, core).
Axes of the slice: x: 4, y: 4 (y_hi: 2, y_lo: 2; y = y_hi * 2 + y_lo), z: 4, core: 2. Of those that a mesh axis runs over, the one named last changes fastest.
Arguments:
- frames: bfloat16 [32, 3, 128, 768], P('tm', None, 'space'), may hold values from -6 to 6
- states: bfloat16 [32, 16, 128, 768], P('tm', None, 'space'), may hold values from -4 to 4
- start_state: bfloat16 [16, 128, 768], P(None, 'space'), may hold values from -4 to 4
- cotangent: bfloat16 [32, 12, 128, 768], P('tm', None, 'space'), may hold values from -6 to 6
- w_rec: bfloat16 [16, 9, 16], replicated, may hold values from -0.1875 to 0.1875
- w_in: bfloat16 [16, 9, 3], replicated, may hold values from -1.25 to 1.25
- bias_vec: float32 [16], replicated, may hold values from -2 to 2
- retain: float32 [16], replicated, may hold values from 0.3 to 0.95
- w_head: bfloat16 [12, 16], replicated, may hold values from -1.5 to 1.5
Outputs:
- grad_rec: float32 [16, 9, 16], replicated
- grad_in: float32 [16, 9, 3], replicated
- grad_bias: float32 [16], replicated
- grad_retain: float32 [16], replicated
- grad_head: float32 [12, 16], replicated
- grad_frames: bfloat16 [32, 3, 128, 768], P('tm', None, 'space')
- boundary_grads: float32 [8, 16, 128, 768], P('tm', None, 'space')
All inputs are finite; a program needn't handle non-finite values.
Results may differ from a plain program's by a relative error of at most 0.0075.
Values may be sent and summed in bfloat16 or wider, within the bound.
A program may use at most 64 MiB of HBM per device.

v0:
```python
import jax
import jax.numpy as jnp
from jax import lax
from jax.sharding import PartitionSpec as P


def shifted(value, axis, steps):
    count = lax.axis_size(axis)
    initial, last = (max(0, -steps), min(count, count - steps))
    return lax.ppermute(value, axis, [(source, source + steps) for source in range(initial, last)])


def with_halo(cells, sides, width):
    for axis, dim in sides:
        count = lax.axis_size(axis)
        ends = count - 1
        head = lax.slice_in_dim(cells, 0, width, axis=dim)
        tail = lax.slice_in_dim(cells, cells.shape[dim] - width, cells.shape[dim], axis=dim)
        cells = jnp.concatenate(
            [
                lax.ppermute(tail, axis, [(i, (i + 1) % count) for i in range(ends)]),
                cells,
                lax.ppermute(head, axis, [((i + 1) % count, i) for i in range(ends)]),
            ],
            axis=dim,
        )
    return cells


def taps_of(padded, row_count, col_count, flipped):
    pieces = []
    for row_step in range(3):
        for col_step in range(3):
            row_at = 2 - row_step if flipped else row_step
            col_at = 2 - col_step if flipped else col_step
            pieces.append(padded[..., row_at : row_at + row_count, col_at : col_at + col_count])
    return jnp.stack(pieces, axis=-4)


def pad_columns(field):
    widths = [(0, 0)] * (field.ndim - 1) + [(1, 1)]
    return jnp.pad(field, widths)


def on_device(frames, states, start_state, cotangent, w_rec, w_in, bias_vec, retain, w_head):
    f32 = jnp.float32
    frame_count = states.shape[0]
    row_count = states.shape[2]
    col_count = states.shape[3]
    tm_count = lax.axis_size("tm")
    position = lax.axis_index("tm")
    earlier = shifted(states[-1], "tm", 1)
    first = jnp.where(position == 0, start_state, earlier)
    previous = jnp.concatenate([first[None], states[:-1]], axis=0)
    prev_rim, frame_rim = (
        with_halo(previous, (("space", 2),), 1),
        with_halo(frames, (("space", 2),), 1),
    )
    prev_taps = taps_of(pad_columns(prev_rim), row_count, col_count, False)
    frame_taps = taps_of(pad_columns(frame_rim), row_count, col_count, False)
    preact = jnp.einsum("okc,fkcrw->forw", w_rec, prev_taps, preferred_element_type=f32)
    preact = preact + jnp.einsum("okc,fkcrw->forw", w_in, frame_taps, preferred_element_type=f32)
    preact = preact + bias_vec[None, :, None, None]
    slopes = 1.0 - jnp.tanh(preact) ** 2
    head_grad = jnp.einsum("forw,fcrw->oc", cotangent, states, preferred_element_type=f32)
    keep_col = retain[:, None, None]
    pushed = jnp.einsum("oc,forw->fcrw", w_head, cotangent, preferred_element_type=f32)
    prev_float = previous.astype(f32)

    def run_block(incoming):
        carried = incoming
        bias_part = jnp.zeros(bias_vec.shape, f32)
        keep_part = jnp.zeros(retain.shape, f32)
        rec_part = jnp.zeros(w_rec.shape, f32)
        in_part = jnp.zeros(w_in.shape, f32)
        kept = [None] * frame_count
        for index in reversed(range(frame_count)):
            gradient = carried + pushed[index]
            dpre = (gradient * slopes[index]).astype(jnp.bfloat16)
            rimmed = pad_columns(with_halo(dpre, (("space", 1),), 1))
            back_taps = taps_of(rimmed, row_count, col_count, True)
            carried = keep_col * gradient + jnp.einsum(
                "okc,korw->crw", w_rec, back_taps, preferred_element_type=f32
            )
            bias_part = bias_part + jnp.sum(dpre.astype(f32), axis=(1, 2))
            keep_part = keep_part + jnp.sum(gradient * prev_float[index], axis=(1, 2))
            rec_part = rec_part + jnp.einsum(
                "orw,kcrw->okc", dpre, prev_taps[index], preferred_element_type=f32
            )
            in_part = in_part + jnp.einsum(
                "orw,kcrw->okc", dpre, frame_taps[index], preferred_element_type=f32
            )
            kept[index] = jnp.einsum("okc,korw->crw", w_in, back_taps, preferred_element_type=f32)
        return (carried, rec_part, in_part, bias_part, keep_part, jnp.stack(kept, axis=0))

    stored = jnp.zeros((frame_count, frames.shape[1], row_count, col_count), f32)
    initial = (
        jnp.zeros(start_state.shape, f32),
        jnp.zeros(w_rec.shape, f32),
        jnp.zeros(w_in.shape, f32),
        jnp.zeros(bias_vec.shape, f32),
        jnp.zeros(retain.shape, f32),
        stored,
    )

    def section(section_no, status):
        received = shifted(status[0], "tm", -1)
        fresh = run_block(received)
        on_turn = position == tm_count - 1 - section_no
        return jax.tree.map(lambda newer, older: jnp.where(on_turn, newer, older), fresh, status)

    final = lax.fori_loop(0, tm_count, section, initial)
    carried_out, rec_grad, in_grad, bias_grad, keep_grad, stored = final
    outgoing = carried_out[None]
    grad_frames = stored.astype(jnp.bfloat16)
    rec_sum, in_sum, bias_sum, keep_sum, head_sum = lax.psum(
        (rec_grad, in_grad, bias_grad, keep_grad, head_grad), ("tm", "space")
    )
    return (rec_sum, in_sum, bias_sum, keep_sum, head_sum, grad_frames, outgoing)


def solution(mesh):
    in_specs = (
        P("tm", None, "space", None),
        P("tm", None, "space", None),
        P(None, "space", None),
        P("tm", None, "space", None),
        P(),
        P(),
        P(),
        P(),
        P(),
    )
    out_specs = (
        P(),
        P(),
        P(),
        P(),
        P(),
        P("tm", None, "space", None),
        P("tm", None, "space", None),
    )
    return jax.shard_map(
        on_device, mesh=mesh, in_specs=in_specs, out_specs=out_specs, check_vma=False
    )
```

profile of v0, /device:TPU:1, one launch (start us, length us, event | category | flops | bytes accessed | tf_op | source)
XLA Modules:
  0.0 679.2 jit_solution(787387750494137866)
XLA Ops:
  1.8 6.2 collective-permute-start.12
  11.2 3.1 collective-permute-start.9
  22.2 10.4 %stack.529 = bf16[4,9,3,8,768]{4,1,2,3,0:T(8,128)(2,1)} concatenate(bf16[4,1,3,8,768]{4,1,2,3,0:T(2,128)(2,1)} %copy.320, bf16[4,1,3,8,768]{4,1,2,3,0:T(2,128)(2,1)S(1)} %copy.321, bf16[4,1,3,8,768]{4,1,2,3,0:T(2,128)(2,1)} %copy.322, bf16[4,1,3,8,768]{4,1,2,3,0:T(2,128)(2,1)} %copy.323, bf16[4,1,3,8,768]{4,1,2,3,0:T(2,128)(2,1)S(1)} %copy.324, ...), dimensions={1} | concatenate | bytes 2654208 | tf_op jit(solution)/shard_map/stack | solution.py:37
  32.6 3.5 copy.332
  37.2 6.0 collective-permute-start.10
  46.4 4.2 collective-permute-done.11
  53.1 3.8 copy.331
  58.6 540.1 %while.26 = (s32[]{:T(128)}, f32[16,8,768]{2,0,1:T(8,128)S(1)}, f32[16,9,16]{2,0,1:T(8,128)S(1)}, f32[16,9,3]{1,0,2:T(8,128)S(1)}, f32[16]{0:T(128)S(1)}, /*inde...) while((s32[]{:T(128)}, f32[16,8,768]{2,0,1:T(8,128)S(1)}, ...), condition=%wide.region_9.10_spmd.clone, body=%wide.region_0.9_spmd.clone.sunk | while | flops 282702208 | bytes 96998152 | solution.py:112
  60.1 7.7 %collective-permute-done = f32[16,8,768]{2,0,1:T(8,128)S(1)} collective-permute-done((f32[16,8,768]{2,0,1:T(8,128)S(1)}, f32[16,8,768]{2,0,1:T(8,128)S(1)}, u32[]{:S(2)}, u32[]{:S(2)}) %collective-permute-start) | collective-permute-done | bytes 393248 | tf_op jit(solution)/shard_map/while/body/eval_jaxpr/ppermute | solution.py:10
  70.9 5.1 collective-permute-start.2
  81.9 5.7 collective-permute-start.4
  87.7 3.5 fusion.317
  99.7 5.1 collective-permute-start.6
  106.8 2.3 fusion.306
  111.7 5.7 collective-permute-start.8
  123.5 8.8 %collective-permute-done = f32[16,8,768]{2,0,1:T(8,128)S(1)} collective-permute-done((f32[16,8,768]{2,0,1:T(8,128)S(1)}, f32[16,8,768]{2,0,1:T(8,128)S(1)}, u32[]{:S(2)}, u32[]{:S(2)}) %collective-permute-start) | collective-permute-done | bytes 393248 | tf_op jit(solution)/shard_map/while/body/eval_jaxpr/ppermute | solution.py:10
  135.4 6.2 collective-permute-start.2
  147.5 5.7 collective-permute-start.4
  153.2 3.5 fusion.317
  165.2 6.2 collective-permute-start.6
  178.4 6.5 collective-permute-start.8
  190.9 8.4 %collective-permute-done = f32[16,8,768]{2,0,1:T(8,128)S(1)} collective-permute-done((f32[16,8,768]{2,0,1:T(8,128)S(1)}, f32[16,8,768]{2,0,1:T(8,128)S(1)}, u32[]{:S(2)}, u32[]{:S(2)}) %collective-permute-start) | collective-permute-done | bytes 393248 | tf_op jit(solution)/shard_map/while/body/eval_jaxpr/ppermute | solution.py:10
  202.5 7.5 %collective-permute-start.2 = (bf16[16,1,768]{2,0,1:T(8,128)(2,1)S(1)}, bf16[16,1,768]{2,0,1:T(8,128)(2,1)S(1)}, u32[]{:S(2)}, u32[]{:S(2)}) collective-permute-start(bf16[16,1,768]{2,0,1:T(8,128)(2,1)S(1)} %get-tuple-element.755), channel_id=1, source_target_pairs={{0,1},{1,2},{2,3},{3,4},{4,5},{5,6},{6,7},{7,8},{8,9},{9,10},{10,1... | collective-permute-start | bytes 73736 | tf_op jit(solution)/shard_map/while/body/eval_jaxpr/ppermute | solution.py:21
  215.8 5.7 collective-permute-start.4
  221.5 3.5 fusion.317
  233.5 6.1 collective-permute-start.6
  241.7 2.3 fusion.306
  246.6 6.5 collective-permute-start.8
  259.2 8.4 %collective-permute-done = f32[16,8,768]{2,0,1:T(8,128)S(1)} collective-permute-done((f32[16,8,768]{2,0,1:T(8,128)S(1)}, f32[16,8,768]{2,0,1:T(8,128)S(1)}, u32[]{:S(2)}, u32[]{:S(2)}) %collective-permute-start) | collective-permute-done | bytes 393248 | tf_op jit(solution)/shard_map/while/body/eval_jaxpr/ppermute | solution.py:10
  270.6 7.5 %collective-permute-start.2 = (bf16[16,1,768]{2,0,1:T(8,128)(2,1)S(1)}, bf16[16,1,768]{2,0,1:T(8,128)(2,1)S(1)}, u32[]{:S(2)}, u32[]{:S(2)}) collective-permute-start(bf16[16,1,768]{2,0,1:T(8,128)(2,1)S(1)} %get-tuple-element.755), channel_id=1, source_target_pairs={{0,1},{1,2},{2,3},{3,4},{4,5},{5,6},{6,7},{7,8},{8,9},{9,10},{10,1... | collective-permute-start | bytes 73736 | tf_op jit(solution)/shard_map/while/body/eval_jaxpr/ppermute | solution.py:21
  284.0 5.7 collective-permute-start.4
  289.7 3.5 fusion.317
  301.7 6.1 collective-permute-start.6
  309.8 2.3 fusion.306
  314.8 6.5 collective-permute-start.8
  327.3 8.4 %collective-permute-done = f32[16,8,768]{2,0,1:T(8,128)S(1)} collective-permute-done((f32[16,8,768]{2,0,1:T(8,128)S(1)}, f32[16,8,768]{2,0,1:T(8,128)S(1)}, u32[]{:S(2)}, u32[]{:S(2)}) %collective-permute-start) | collective-permute-done | bytes 393248 | tf_op jit(solution)/shard_map/while/body/eval_jaxpr/ppermute | solution.py:10
  338.8 7.5 %collective-permute-start.2 = (bf16[16,1,768]{2,0,1:T(8,128)(2,1)S(1)}, bf16[16,1,768]{2,0,1:T(8,128)(2,1)S(1)}, u32[]{:S(2)}, u32[]{:S(2)}) collective-permute-start(bf16[16,1,768]{2,0,1:T(8,128)(2,1)S(1)} %get-tuple-element.755), channel_id=1, source_target_pairs={{0,1},{1,2},{2,3},{3,4},{4,5},{5,6},{6,7},{7,8},{8,9},{9,10},{10,1... | collective-permute-start | bytes 73736 | tf_op jit(solution)/shard_map/while/body/eval_jaxpr/ppermute | solution.py:21
  352.1 5.7 collective-permute-start.4
  357.9 3.5 fusion.317
  369.9 6.1 collective-permute-start.6
  378.0 2.3 fusion.306
  382.9 6.5 collective-permute-start.8
  395.5 8.4 %collective-permute-done = f32[16,8,768]{2,0,1:T(8,128)S(1)} collective-permute-done((f32[16,8,768]{2,0,1:T(8,128)S(1)}, f32[16,8,768]{2,0,1:T(8,128)S(1)}, u32[]{:S(2)}, u32[]{:S(2)}) %collective-permute-start) | collective-permute-done | bytes 393248 | tf_op jit(solution)/shard_map/while/body/eval_jaxpr/ppermute | solution.py:10
  407.0 7.5 %collective-permute-start.2 = (bf16[16,1,768]{2,0,1:T(8,128)(2,1)S(1)}, bf16[16,1,768]{2,0,1:T(8,128)(2,1)S(1)}, u32[]{:S(2)}, u32[]{:S(2)}) collective-permute-start(bf16[16,1,768]{2,0,1:T(8,128)(2,1)S(1)} %get-tuple-element.755), channel_id=1, source_target_pairs={{0,1},{1,2},{2,3},{3,4},{4,5},{5,6},{6,7},{7,8},{8,9},{9,10},{10,1... | collective-permute-start | bytes 73736 | tf_op jit(solution)/shard_map/while/body/eval_jaxpr/ppermute | solution.py:21
  420.3 5.7 collective-permute-start.4
  426.0 3.5 fusion.317
  438.0 6.1 collective-permute-start.6
  446.2 2.3 fusion.306
  451.1 6.5 collective-permute-start.8
  463.7 8.4 %collective-permute-done = f32[16,8,768]{2,0,1:T(8,128)S(1)} collective-permute-done((f32[16,8,768]{2,0,1:T(8,128)S(1)}, f32[16,8,768]{2,0,1:T(8,128)S(1)}, u32[]{:S(2)}, u32[]{:S(2)}) %collective-permute-start) | collective-permute-done | bytes 393248 | tf_op jit(solution)/shard_map/while/body/eval_jaxpr/ppermute | solution.py:10
  475.1 7.5 %collective-permute-start.2 = (bf16[16,1,768]{2,0,1:T(8,128)(2,1)S(1)}, bf16[16,1,768]{2,0,1:T(8,128)(2,1)S(1)}, u32[]{:S(2)}, u32[]{:S(2)}) collective-permute-start(bf16[16,1,768]{2,0,1:T(8,128)(2,1)S(1)} %get-tuple-element.755), channel_id=1, source_target_pairs={{0,1},{1,2},{2,3},{3,4},{4,5},{5,6},{6,7},{7,8},{8,9},{9,10},{10,1... | collective-permute-start | bytes 73736 | tf_op jit(solution)/shard_map/while/body/eval_jaxpr/ppermute | solution.py:21
  488.5 5.7 collective-permute-start.4
  494.2 3.5 fusion.317
  506.2 6.1 collective-permute-start.6
  514.3 2.3 fusion.306
  519.3 6.5 collective-permute-start.8
  531.8 8.4 %collective-permute-done = f32[16,8,768]{2,0,1:T(8,128)S(1)} collective-permute-done((f32[16,8,768]{2,0,1:T(8,128)S(1)}, f32[16,8,768]{2,0,1:T(8,128)S(1)}, u32[]{:S(2)}, u32[]{:S(2)}) %collective-permute-start) | collective-permute-done | bytes 393248 | tf_op jit(solution)/shard_map/while/body/eval_jaxpr/ppermute | solution.py:10
  543.3 7.5 %collective-permute-start.2 = (bf16[16,1,768]{2,0,1:T(8,128)(2,1)S(1)}, bf16[16,1,768]{2,0,1:T(8,128)(2,1)S(1)}, u32[]{:S(2)}, u32[]{:S(2)}) collective-permute-start(bf16[16,1,768]{2,0,1:T(8,128)(2,1)S(1)} %get-tuple-element.755), channel_id=1, source_target_pairs={{0,1},{1,2},{2,3},{3,4},{4,5},{5,6},{6,7},{7,8},{8,9},{9,10},{10,1... | collective-permute-start | bytes 73736 | tf_op jit(solution)/shard_map/while/body/eval_jaxpr/ppermute | solution.py:21
  556.6 5.7 collective-permute-start.4
  562.4 3.5 fusion.317
  574.4 6.1 collective-permute-start.6
  582.5 2.3 fusion.306
  587.4 6.5 collective-permute-start.8
  600.4 78.8 %all-reduce.6 = (f32[16,9,16]{2,0,1:T(8,128)}, f32[16,9,3]{0,2,1:T(4,128)}, f32[16]{0:T(128)}, f32[16]{0:T(128)}, f32[12,16]{1,0:T(8,128)}) all-reduce(f32[16,9,16]{2,0,1:T(8,128)S(1)} %get-tuple-element.386, f32[16,9,3]{0,2,1:T(4,128)S(1)} %copy.333, ...), channel_id=1, replica_groups=mesh['tm'=8,'space'=16] {'tm','space'}, use_global_device_ids=true, to_apply=%region_10.11 | all-reduce | flops 2960 | bytes 23680 | tf_op jit(solution)/shard_map/psum | solution.py:116
  (726 shorter events, 245.5 us)
Async XLA Ops:
  1.8 15.6 %collective-permute-start.12 = (bf16[4,3,1,768]{3,2,1,0:T(2,128)(2,1)S(1)}, bf16[4,3,1,768]{3,2,1,0:T(2,128)(2,1)S(1)}, u32[]{:S(2)}, u32[]{:S(2)}) collective-permute-start(bf16[4,3,1,768]{3,2,1,0:T(2,128)(2,1)S(1)} %get-tuple-element.629), channel_id=1, source_target_pairs={{0,1},{1,2},{2,3},{3,4},{4,5},{5,6},{6,7},{7,8},{8,9},{9,10},{10,1... | collective-permute-start | bytes 55304 | tf_op jit(solution)/shard_map/ppermute | solution.py:21
  8.0 9.4 %collective-permute-start.13 = (bf16[4,3,1,768]{3,2,1,0:T(2,128)(2,1)S(1)}, bf16[4,3,1,768]{3,2,1,0:T(2,128)(2,1)S(1)}, u32[]{:S(2)}, u32[]{:S(2)}) collective-permute-start(bf16[4,3,1,768]{3,2,1,0:T(2,128)(2,1)S(1)} %get-tuple-element.630), channel_id=1, source_target_pairs={{1,0},{2,1},{3,2},{4,3},{5,4},{6,5},{7,6},{8,7},{9,8},{10,9},{11,1... | collective-permute-start | bytes 55304 | tf_op jit(solution)/shard_map/ppermute | solution.py:23
  11.2 25.4 %collective-permute-start.9 = (bf16[16,8,768]{2,0,1:T(8,128)(2,1)S(1)}, bf16[16,8,768]{2,0,1:T(8,128)(2,1)}, u32[]{:S(2)}, u32[]{:S(2)}) collective-permute-start(bf16[16,8,768]{2,0,1:T(8,128)(2,1)S(1)} %slice_bitcast_fusion.30), channel_id=1, source_target_pairs={{0,16},{16,32},{32,48},{48,64},{64,80},{80,96},{96,112},{1,17},{17... | collective-permute-start | bytes 589832 | tf_op jit(solution)/shard_map/ppermute | solution.py:10
  37.2 9.2 %collective-permute-start.10 = (bf16[4,16,1,768]{3,1,2,0:T(8,128)(2,1)S(1)}, bf16[4,16,1,768]{3,1,2,0:T(8,128)(2,1)S(1)}, u32[]{:S(2)}, u32[]{:S(2)}) collective-permute-start(bf16[4,16,1,768]{3,1,2,0:T(8,128)(2,1)S(1)} %get-tuple-element.619), channel_id=1, source_target_pairs={{0,1},{1,2},{2,3},{3,4},{4,5},{5,6},{6,7},{7,8},{8,9},{9,10},{10,1... | collective-permute-start | bytes 294920 | tf_op jit(solution)/shard_map/ppermute | solution.py:21
  58.8 9.0 %collective-permute-start = (f32[16,8,768]{2,0,1:T(8,128)S(1)}, f32[16,8,768]{2,0,1:T(8,128)S(1)}, u32[]{:S(2)}, u32[]{:S(2)}) collective-permute-start(f32[16,8,768]{2,0,1:T(8,128)S(1)} %broadcast_select_fusion.7), channel_id=1, source_target_pairs={{16,0},{32,16},{48,32},{64,48},{80,64},{96,80},{112,96},{17,1},{33... | collective-permute-start | bytes 1179656 | tf_op jit(solution)/shard_map/while/body/eval_jaxpr/ppermute | solution.py:10
  79.9 14.0 %collective-permute-start.3 = (bf16[16,1,768]{2,0,1:T(8,128)(2,1)S(1)}, bf16[16,1,768]{2,0,1:T(8,128)(2,1)S(1)}, u32[]{:S(2)}, u32[]{:S(2)}) collective-permute-start(bf16[16,1,768]{2,0,1:T(8,128)(2,1)S(1)} %get-tuple-element.758), channel_id=1, source_target_pairs={{1,0},{2,1},{3,2},{4,3},{5,4},{6,5},{7,6},{8,7},{9,8},{10,9},{11,1... | collective-permute-start | bytes 73736 | tf_op jit(solution)/shard_map/while/body/eval_jaxpr/ppermute | solution.py:23
  81.9 11.9 %collective-permute-start.4 = (bf16[16,1,768]{2,0,1:T(8,128)(2,1)S(1)}, bf16[16,1,768]{2,0,1:T(8,128)(2,1)S(1)}, u32[]{:S(2)}, u32[]{:S(2)}) collective-permute-start(bf16[16,1,768]{2,0,1:T(8,128)(2,1)S(1)} %get-tuple-element.759), channel_id=1, source_target_pairs={{0,1},{1,2},{2,3},{3,4},{4,5},{5,6},{6,7},{7,8},{8,9},{9,10},{10,1... | collective-permute-start | bytes 73736 | tf_op jit(solution)/shard_map/while/body/eval_jaxpr/ppermute | solution.py:21
  109.8 10.4 %collective-permute-start.7 = (bf16[16,1,768]{2,0,1:T(8,128)(2,1)S(1)}, bf16[16,1,768]{2,0,1:T(8,128)(2,1)S(1)}, u32[]{:S(2)}, u32[]{:S(2)}) collective-permute-start(bf16[16,1,768]{2,0,1:T(8,128)(2,1)S(1)} %get-tuple-element.765), channel_id=1, source_target_pairs={{1,0},{2,1},{3,2},{4,3},{5,4},{6,5},{7,6},{8,7},{9,8},{10,9},{11,1... | collective-permute-start | bytes 73736 | tf_op jit(solution)/shard_map/while/body/eval_jaxpr/ppermute | solution.py:23
  111.7 8.4 %collective-permute-start.8 = (bf16[16,1,768]{2,0,1:T(8,128)(2,1)S(1)}, bf16[16,1,768]{2,0,1:T(8,128)(2,1)S(1)}, u32[]{:S(2)}, u32[]{:S(2)}) collective-permute-start(bf16[16,1,768]{2,0,1:T(8,128)(2,1)S(1)} %get-tuple-element.766), channel_id=1, source_target_pairs={{0,1},{1,2},{2,3},{3,4},{4,5},{5,6},{6,7},{7,8},{8,9},{9,10},{10,1... | collective-permute-start | bytes 73736 | tf_op jit(solution)/shard_map/while/body/eval_jaxpr/ppermute | solution.py:21
  122.2 10.1 %collective-permute-start = (f32[16,8,768]{2,0,1:T(8,128)S(1)}, f32[16,8,768]{2,0,1:T(8,128)S(1)}, u32[]{:S(2)}, u32[]{:S(2)}) collective-permute-start(f32[16,8,768]{2,0,1:T(8,128)S(1)} %broadcast_select_fusion.7), channel_id=1, source_target_pairs={{16,0},{32,16},{48,32},{64,48},{80,64},{96,80},{112,96},{17,1},{33... | collective-permute-start | bytes 1179656 | tf_op jit(solution)/shard_map/while/body/eval_jaxpr/ppermute | solution.py:10
  133.5 8.2 %collective-permute-start.1 = (bf16[16,1,768]{2,0,1:T(8,128)(2,1)S(1)}, bf16[16,1,768]{2,0,1:T(8,128)(2,1)S(1)}, u32[]{:S(2)}, u32[]{:S(2)}) collective-permute-start(bf16[16,1,768]{2,0,1:T(8,128)(2,1)S(1)} %get-tuple-element.754), channel_id=1, source_target_pairs={{1,0},{2,1},{3,2},{4,3},{5,4},{6,5},{7,6},{8,7},{9,8},{10,9},{11,1... | collective-permute-start | bytes 73736 | tf_op jit(solution)/shard_map/while/body/eval_jaxpr/ppermute | solution.py:23
  145.4 14.0 %collective-permute-start.3 = (bf16[16,1,768]{2,0,1:T(8,128)(2,1)S(1)}, bf16[16,1,768]{2,0,1:T(8,128)(2,1)S(1)}, u32[]{:S(2)}, u32[]{:S(2)}) collective-permute-start(bf16[16,1,768]{2,0,1:T(8,128)(2,1)S(1)} %get-tuple-element.758), channel_id=1, source_target_pairs={{1,0},{2,1},{3,2},{4,3},{5,4},{6,5},{7,6},{8,7},{9,8},{10,9},{11,1... | collective-permute-start | bytes 73736 | tf_op jit(solution)/shard_map/while/body/eval_jaxpr/ppermute | solution.py:23
  147.5 11.9 %collective-permute-start.4 = (bf16[16,1,768]{2,0,1:T(8,128)(2,1)S(1)}, bf16[16,1,768]{2,0,1:T(8,128)(2,1)S(1)}, u32[]{:S(2)}, u32[]{:S(2)}) collective-permute-start(bf16[16,1,768]{2,0,1:T(8,128)(2,1)S(1)} %get-tuple-element.759), channel_id=1, source_target_pairs={{0,1},{1,2},{2,3},{3,4},{4,5},{5,6},{6,7},{7,8},{8,9},{9,10},{10,1... | collective-permute-start | bytes 73736 | tf_op jit(solution)/shard_map/while/body/eval_jaxpr/ppermute | solution.py:21
  163.3 8.8 %collective-permute-start.5 = (bf16[16,1,768]{2,0,1:T(8,128)(2,1)S(1)}, bf16[16,1,768]{2,0,1:T(8,128)(2,1)S(1)}, u32[]{:S(2)}, u32[]{:S(2)}) collective-permute-start(bf16[16,1,768]{2,0,1:T(8,128)(2,1)S(1)} %get-tuple-element.762), channel_id=1, source_target_pairs={{1,0},{2,1},{3,2},{4,3},{5,4},{6,5},{7,6},{8,7},{9,8},{10,9},{11,1... | collective-permute-start | bytes 73736 | tf_op jit(solution)/shard_map/while/body/eval_jaxpr/ppermute | solution.py:23
  176.4 11.2 %collective-permute-start.7 = (bf16[16,1,768]{2,0,1:T(8,128)(2,1)S(1)}, bf16[16,1,768]{2,0,1:T(8,128)(2,1)S(1)}, u32[]{:S(2)}, u32[]{:S(2)}) collective-permute-start(bf16[16,1,768]{2,0,1:T(8,128)(2,1)S(1)} %get-tuple-element.765), channel_id=1, source_target_pairs={{1,0},{2,1},{3,2},{4,3},{5,4},{6,5},{7,6},{8,7},{9,8},{10,9},{11,1... | collective-permute-start | bytes 73736 | tf_op jit(solution)/shard_map/while/body/eval_jaxpr/ppermute | solution.py:23
  178.4 9.2 %collective-permute-start.8 = (bf16[16,1,768]{2,0,1:T(8,128)(2,1)S(1)}, bf16[16,1,768]{2,0,1:T(8,128)(2,1)S(1)}, u32[]{:S(2)}, u32[]{:S(2)}) collective-permute-start(bf16[16,1,768]{2,0,1:T(8,128)(2,1)S(1)} %get-tuple-element.766), channel_id=1, source_target_pairs={{0,1},{1,2},{2,3},{3,4},{4,5},{5,6},{6,7},{7,8},{8,9},{9,10},{10,1... | collective-permute-start | bytes 73736 | tf_op jit(solution)/shard_map/while/body/eval_jaxpr/ppermute | solution.py:21
  189.6 9.7 %collective-permute-start = (f32[16,8,768]{2,0,1:T(8,128)S(1)}, f32[16,8,768]{2,0,1:T(8,128)S(1)}, u32[]{:S(2)}, u32[]{:S(2)}) collective-permute-start(f32[16,8,768]{2,0,1:T(8,128)S(1)} %broadcast_select_fusion.7), channel_id=1, source_target_pairs={{16,0},{32,16},{48,32},{64,48},{80,64},{96,80},{112,96},{17,1},{33... | collective-permute-start | bytes 1179656 | tf_op jit(solution)/shard_map/while/body/eval_jaxpr/ppermute | solution.py:10
  200.5 9.4 %collective-permute-start.1 = (bf16[16,1,768]{2,0,1:T(8,128)(2,1)S(1)}, bf16[16,1,768]{2,0,1:T(8,128)(2,1)S(1)}, u32[]{:S(2)}, u32[]{:S(2)}) collective-permute-start(bf16[16,1,768]{2,0,1:T(8,128)(2,1)S(1)} %get-tuple-element.754), channel_id=1, source_target_pairs={{1,0},{2,1},{3,2},{4,3},{5,4},{6,5},{7,6},{8,7},{9,8},{10,9},{11,1... | collective-permute-start | bytes 73736 | tf_op jit(solution)/shard_map/while/body/eval_jaxpr/ppermute | solution.py:23
  202.5 8.4 %collective-permute-start.2 = (bf16[16,1,768]{2,0,1:T(8,128)(2,1)S(1)}, bf16[16,1,768]{2,0,1:T(8,128)(2,1)S(1)}, u32[]{:S(2)}, u32[]{:S(2)}) collective-permute-start(bf16[16,1,768]{2,0,1:T(8,128)(2,1)S(1)} %get-tuple-element.755), channel_id=1, source_target_pairs={{0,1},{1,2},{2,3},{3,4},{4,5},{5,6},{6,7},{7,8},{8,9},{9,10},{10,1... | collective-permute-start | bytes 73736 | tf_op jit(solution)/shard_map/while/body/eval_jaxpr/ppermute | solution.py:21
  213.7 14.0 %collective-permute-start.3 = (bf16[16,1,768]{2,0,1:T(8,128)(2,1)S(1)}, bf16[16,1,768]{2,0,1:T(8,128)(2,1)S(1)}, u32[]{:S(2)}, u32[]{:S(2)}) collective-permute-start(bf16[16,1,768]{2,0,1:T(8,128)(2,1)S(1)} %get-tuple-element.758), channel_id=1, source_target_pairs={{1,0},{2,1},{3,2},{4,3},{5,4},{6,5},{7,6},{8,7},{9,8},{10,9},{11,1... | collective-permute-start | bytes 73736 | tf_op jit(solution)/shard_map/while/body/eval_jaxpr/ppermute | solution.py:23
  215.8 11.9 %collective-permute-start.4 = (bf16[16,1,768]{2,0,1:T(8,128)(2,1)S(1)}, bf16[16,1,768]{2,0,1:T(8,128)(2,1)S(1)}, u32[]{:S(2)}, u32[]{:S(2)}) collective-permute-start(bf16[16,1,768]{2,0,1:T(8,128)(2,1)S(1)} %get-tuple-element.759), channel_id=1, source_target_pairs={{0,1},{1,2},{2,3},{3,4},{4,5},{5,6},{6,7},{7,8},{8,9},{9,10},{10,1... | collective-permute-start | bytes 73736 | tf_op jit(solution)/shard_map/while/body/eval_jaxpr/ppermute | solution.py:21
  231.6 8.7 %collective-permute-start.5 = (bf16[16,1,768]{2,0,1:T(8,128)(2,1)S(1)}, bf16[16,1,768]{2,0,1:T(8,128)(2,1)S(1)}, u32[]{:S(2)}, u32[]{:S(2)}) collective-permute-start(bf16[16,1,768]{2,0,1:T(8,128)(2,1)S(1)} %get-tuple-element.762), channel_id=1, source_target_pairs={{1,0},{2,1},{3,2},{4,3},{5,4},{6,5},{7,6},{8,7},{9,8},{10,9},{11,1... | collective-permute-start | bytes 73736 | tf_op jit(solution)/shard_map/while/body/eval_jaxpr/ppermute | solution.py:23
  244.6 11.2 %collective-permute-start.7 = (bf16[16,1,768]{2,0,1:T(8,128)(2,1)S(1)}, bf16[16,1,768]{2,0,1:T(8,128)(2,1)S(1)}, u32[]{:S(2)}, u32[]{:S(2)}) collective-permute-start(bf16[16,1,768]{2,0,1:T(8,128)(2,1)S(1)} %get-tuple-element.765), channel_id=1, source_target_pairs={{1,0},{2,1},{3,2},{4,3},{5,4},{6,5},{7,6},{8,7},{9,8},{10,9},{11,1... | collective-permute-start | bytes 73736 | tf_op jit(solution)/shard_map/while/body/eval_jaxpr/ppermute | solution.py:23
  246.6 9.2 %collective-permute-start.8 = (bf16[16,1,768]{2,0,1:T(8,128)(2,1)S(1)}, bf16[16,1,768]{2,0,1:T(8,128)(2,1)S(1)}, u32[]{:S(2)}, u32[]{:S(2)}) collective-permute-start(bf16[16,1,768]{2,0,1:T(8,128)(2,1)S(1)} %get-tuple-element.766), channel_id=1, source_target_pairs={{0,1},{1,2},{2,3},{3,4},{4,5},{5,6},{6,7},{7,8},{8,9},{9,10},{10,1... | collective-permute-start | bytes 73736 | tf_op jit(solution)/shard_map/while/body/eval_jaxpr/ppermute | solution.py:21
  257.9 9.7 %collective-permute-start = (f32[16,8,768]{2,0,1:T(8,128)S(1)}, f32[16,8,768]{2,0,1:T(8,128)S(1)}, u32[]{:S(2)}, u32[]{:S(2)}) collective-permute-start(f32[16,8,768]{2,0,1:T(8,128)S(1)} %broadcast_select_fusion.7), channel_id=1, source_target_pairs={{16,0},{32,16},{48,32},{64,48},{80,64},{96,80},{112,96},{17,1},{33... | collective-permute-start | bytes 1179656 | tf_op jit(solution)/shard_map/while/body/eval_jaxpr/ppermute | solution.py:10
  268.7 9.4 %collective-permute-start.1 = (bf16[16,1,768]{2,0,1:T(8,128)(2,1)S(1)}, bf16[16,1,768]{2,0,1:T(8,128)(2,1)S(1)}, u32[]{:S(2)}, u32[]{:S(2)}) collective-permute-start(bf16[16,1,768]{2,0,1:T(8,128)(2,1)S(1)} %get-tuple-element.754), channel_id=1, source_target_pairs={{1,0},{2,1},{3,2},{4,3},{5,4},{6,5},{7,6},{8,7},{9,8},{10,9},{11,1... | collective-permute-start | bytes 73736 | tf_op jit(solution)/shard_map/while/body/eval_jaxpr/ppermute | solution.py:23
  270.6 8.4 %collective-permute-start.2 = (bf16[16,1,768]{2,0,1:T(8,128)(2,1)S(1)}, bf16[16,1,768]{2,0,1:T(8,128)(2,1)S(1)}, u32[]{:S(2)}, u32[]{:S(2)}) collective-permute-start(bf16[16,1,768]{2,0,1:T(8,128)(2,1)S(1)} %get-tuple-element.755), channel_id=1, source_target_pairs={{0,1},{1,2},{2,3},{3,4},{4,5},{5,6},{6,7},{7,8},{8,9},{9,10},{10,1... | collective-permute-start | bytes 73736 | tf_op jit(solution)/shard_map/while/body/eval_jaxpr/ppermute | solution.py:21
  281.9 14.0 %collective-permute-start.3 = (bf16[16,1,768]{2,0,1:T(8,128)(2,1)S(1)}, bf16[16,1,768]{2,0,1:T(8,128)(2,1)S(1)}, u32[]{:S(2)}, u32[]{:S(2)}) collective-permute-start(bf16[16,1,768]{2,0,1:T(8,128)(2,1)S(1)} %get-tuple-element.758), channel_id=1, source_target_pairs={{1,0},{2,1},{3,2},{4,3},{5,4},{6,5},{7,6},{8,7},{9,8},{10,9},{11,1... | collective-permute-start | bytes 73736 | tf_op jit(solution)/shard_map/while/body/eval_jaxpr/ppermute | solution.py:23
  284.0 11.9 %collective-permute-start.4 = (bf16[16,1,768]{2,0,1:T(8,128)(2,1)S(1)}, bf16[16,1,768]{2,0,1:T(8,128)(2,1)S(1)}, u32[]{:S(2)}, u32[]{:S(2)}) collective-permute-start(bf16[16,1,768]{2,0,1:T(8,128)(2,1)S(1)} %get-tuple-element.759), channel_id=1, source_target_pairs={{0,1},{1,2},{2,3},{3,4},{4,5},{5,6},{6,7},{7,8},{8,9},{9,10},{10,1... | collective-permute-start | bytes 73736 | tf_op jit(solution)/shard_map/while/body/eval_jaxpr/ppermute | solution.py:21
  299.8 8.7 %collective-permute-start.5 = (bf16[16,1,768]{2,0,1:T(8,128)(2,1)S(1)}, bf16[16,1,768]{2,0,1:T(8,128)(2,1)S(1)}, u32[]{:S(2)}, u32[]{:S(2)}) collective-permute-start(bf16[16,1,768]{2,0,1:T(8,128)(2,1)S(1)} %get-tuple-element.762), channel_id=1, source_target_pairs={{1,0},{2,1},{3,2},{4,3},{5,4},{6,5},{7,6},{8,7},{9,8},{10,9},{11,1... | collective-permute-start | bytes 73736 | tf_op jit(solution)/shard_map/while/body/eval_jaxpr/ppermute | solution.py:23
  312.8 11.2 %collective-permute-start.7 = (bf16[16,1,768]{2,0,1:T(8,128)(2,1)S(1)}, bf16[16,1,768]{2,0,1:T(8,128)(2,1)S(1)}, u32[]{:S(2)}, u32[]{:S(2)}) collective-permute-start(bf16[16,1,768]{2,0,1:T(8,128)(2,1)S(1)} %get-tuple-element.765), channel_id=1, source_target_pairs={{1,0},{2,1},{3,2},{4,3},{5,4},{6,5},{7,6},{8,7},{9,8},{10,9},{11,1... | collective-permute-start | bytes 73736 | tf_op jit(solution)/shard_map/while/body/eval_jaxpr/ppermute | solution.py:23
  314.8 9.2 %collective-permute-start.8 = (bf16[16,1,768]{2,0,1:T(8,128)(2,1)S(1)}, bf16[16,1,768]{2,0,1:T(8,128)(2,1)S(1)}, u32[]{:S(2)}, u32[]{:S(2)}) collective-permute-start(bf16[16,1,768]{2,0,1:T(8,128)(2,1)S(1)} %get-tuple-element.766), channel_id=1, source_target_pairs={{0,1},{1,2},{2,3},{3,4},{4,5},{5,6},{6,7},{7,8},{8,9},{9,10},{10,1... | collective-permute-start | bytes 73736 | tf_op jit(solution)/shard_map/while/body/eval_jaxpr/ppermute | solution.py:21
  326.0 9.7 %collective-permute-start = (f32[16,8,768]{2,0,1:T(8,128)S(1)}, f32[16,8,768]{2,0,1:T(8,128)S(1)}, u32[]{:S(2)}, u32[]{:S(2)}) collective-permute-start(f32[16,8,768]{2,0,1:T(8,128)S(1)} %broadcast_select_fusion.7), channel_id=1, source_target_pairs={{16,0},{32,16},{48,32},{64,48},{80,64},{96,80},{112,96},{17,1},{33... | collective-permute-start | bytes 1179656 | tf_op jit(solution)/shard_map/while/body/eval_jaxpr/ppermute | solution.py:10
  336.9 9.4 %collective-permute-start.1 = (bf16[16,1,768]{2,0,1:T(8,128)(2,1)S(1)}, bf16[16,1,768]{2,0,1:T(8,128)(2,1)S(1)}, u32[]{:S(2)}, u32[]{:S(2)}) collective-permute-start(bf16[16,1,768]{2,0,1:T(8,128)(2,1)S(1)} %get-tuple-element.754), channel_id=1, source_target_pairs={{1,0},{2,1},{3,2},{4,3},{5,4},{6,5},{7,6},{8,7},{9,8},{10,9},{11,1... | collective-permute-start | bytes 73736 | tf_op jit(solution)/shard_map/while/body/eval_jaxpr/ppermute | solution.py:23
  338.8 8.4 %collective-permute-start.2 = (bf16[16,1,768]{2,0,1:T(8,128)(2,1)S(1)}, bf16[16,1,768]{2,0,1:T(8,128)(2,1)S(1)}, u32[]{:S(2)}, u32[]{:S(2)}) collective-permute-start(bf16[16,1,768]{2,0,1:T(8,128)(2,1)S(1)} %get-tuple-element.755), channel_id=1, source_target_pairs={{0,1},{1,2},{2,3},{3,4},{4,5},{5,6},{6,7},{7,8},{8,9},{9,10},{10,1... | collective-permute-start | bytes 73736 | tf_op jit(solution)/shard_map/while/body/eval_jaxpr/ppermute | solution.py:21
  350.1 14.0 %collective-permute-start.3 = (bf16[16,1,768]{2,0,1:T(8,128)(2,1)S(1)}, bf16[16,1,768]{2,0,1:T(8,128)(2,1)S(1)}, u32[]{:S(2)}, u32[]{:S(2)}) collective-permute-start(bf16[16,1,768]{2,0,1:T(8,128)(2,1)S(1)} %get-tuple-element.758), channel_id=1, source_target_pairs={{1,0},{2,1},{3,2},{4,3},{5,4},{6,5},{7,6},{8,7},{9,8},{10,9},{11,1... | collective-permute-start | bytes 73736 | tf_op jit(solution)/shard_map/while/body/eval_jaxpr/ppermute | solution.py:23
  352.1 11.9 %collective-permute-start.4 = (bf16[16,1,768]{2,0,1:T(8,128)(2,1)S(1)}, bf16[16,1,768]{2,0,1:T(8,128)(2,1)S(1)}, u32[]{:S(2)}, u32[]{:S(2)}) collective-permute-start(bf16[16,1,768]{2,0,1:T(8,128)(2,1)S(1)} %get-tuple-element.759), channel_id=1, source_target_pairs={{0,1},{1,2},{2,3},{3,4},{4,5},{5,6},{6,7},{7,8},{8,9},{9,10},{10,1... | collective-permute-start | bytes 73736 | tf_op jit(solution)/shard_map/while/body/eval_jaxpr/ppermute | solution.py:21
  367.9 8.7 %collective-permute-start.5 = (bf16[16,1,768]{2,0,1:T(8,128)(2,1)S(1)}, bf16[16,1,768]{2,0,1:T(8,128)(2,1)S(1)}, u32[]{:S(2)}, u32[]{:S(2)}) collective-permute-start(bf16[16,1,768]{2,0,1:T(8,128)(2,1)S(1)} %get-tuple-element.762), channel_id=1, source_target_pairs={{1,0},{2,1},{3,2},{4,3},{5,4},{6,5},{7,6},{8,7},{9,8},{10,9},{11,1... | collective-permute-start | bytes 73736 | tf_op jit(solution)/shard_map/while/body/eval_jaxpr/ppermute | solution.py:23
  381.0 11.2 %collective-permute-start.7 = (bf16[16,1,768]{2,0,1:T(8,128)(2,1)S(1)}, bf16[16,1,768]{2,0,1:T(8,128)(2,1)S(1)}, u32[]{:S(2)}, u32[]{:S(2)}) collective-permute-start(bf16[16,1,768]{2,0,1:T(8,128)(2,1)S(1)} %get-tuple-element.765), channel_id=1, source_target_pairs={{1,0},{2,1},{3,2},{4,3},{5,4},{6,5},{7,6},{8,7},{9,8},{10,9},{11,1... | collective-permute-start | bytes 73736 | tf_op jit(solution)/shard_map/while/body/eval_jaxpr/ppermute | solution.py:23
  382.9 9.2 %collective-permute-start.8 = (bf16[16,1,768]{2,0,1:T(8,128)(2,1)S(1)}, bf16[16,1,768]{2,0,1:T(8,128)(2,1)S(1)}, u32[]{:S(2)}, u32[]{:S(2)}) collective-permute-start(bf16[16,1,768]{2,0,1:T(8,128)(2,1)S(1)} %get-tuple-element.766), channel_id=1, source_target_pairs={{0,1},{1,2},{2,3},{3,4},{4,5},{5,6},{6,7},{7,8},{8,9},{9,10},{10,1... | collective-permute-start | bytes 73736 | tf_op jit(solution)/shard_map/while/body/eval_jaxpr/ppermute | solution.py:21
  394.2 9.7 %collective-permute-start = (f32[16,8,768]{2,0,1:T(8,128)S(1)}, f32[16,8,768]{2,0,1:T(8,128)S(1)}, u32[]{:S(2)}, u32[]{:S(2)}) collective-permute-start(f32[16,8,768]{2,0,1:T(8,128)S(1)} %broadcast_select_fusion.7), channel_id=1, source_target_pairs={{16,0},{32,16},{48,32},{64,48},{80,64},{96,80},{112,96},{17,1},{33... | collective-permute-start | bytes 1179656 | tf_op jit(solution)/shard_map/while/body/eval_jaxpr/ppermute | solution.py:10
  405.0 9.4 %collective-permute-start.1 = (bf16[16,1,768]{2,0,1:T(8,128)(2,1)S(1)}, bf16[16,1,768]{2,0,1:T(8,128)(2,1)S(1)}, u32[]{:S(2)}, u32[]{:S(2)}) collective-permute-start(bf16[16,1,768]{2,0,1:T(8,128)(2,1)S(1)} %get-tuple-element.754), channel_id=1, source_target_pairs={{1,0},{2,1},{3,2},{4,3},{5,4},{6,5},{7,6},{8,7},{9,8},{10,9},{11,1... | collective-permute-start | bytes 73736 | tf_op jit(solution)/shard_map/while/body/eval_jaxpr/ppermute | solution.py:23
  407.0 8.4 %collective-permute-start.2 = (bf16[16,1,768]{2,0,1:T(8,128)(2,1)S(1)}, bf16[16,1,768]{2,0,1:T(8,128)(2,1)S(1)}, u32[]{:S(2)}, u32[]{:S(2)}) collective-permute-start(bf16[16,1,768]{2,0,1:T(8,128)(2,1)S(1)} %get-tuple-element.755), channel_id=1, source_target_pairs={{0,1},{1,2},{2,3},{3,4},{4,5},{5,6},{6,7},{7,8},{8,9},{9,10},{10,1... | collective-permute-start | bytes 73736 | tf_op jit(solution)/shard_map/while/body/eval_jaxpr/ppermute | solution.py:21
  418.3 14.0 %collective-permute-start.3 = (bf16[16,1,768]{2,0,1:T(8,128)(2,1)S(1)}, bf16[16,1,768]{2,0,1:T(8,128)(2,1)S(1)}, u32[]{:S(2)}, u32[]{:S(2)}) collective-permute-start(bf16[16,1,768]{2,0,1:T(8,128)(2,1)S(1)} %get-tuple-element.758), channel_id=1, source_target_pairs={{1,0},{2,1},{3,2},{4,3},{5,4},{6,5},{7,6},{8,7},{9,8},{10,9},{11,1... | collective-permute-start | bytes 73736 | tf_op jit(solution)/shard_map/while/body/eval_jaxpr/ppermute | solution.py:23
  420.3 11.9 %collective-permute-start.4 = (bf16[16,1,768]{2,0,1:T(8,128)(2,1)S(1)}, bf16[16,1,768]{2,0,1:T(8,128)(2,1)S(1)}, u32[]{:S(2)}, u32[]{:S(2)}) collective-permute-start(bf16[16,1,768]{2,0,1:T(8,128)(2,1)S(1)} %get-tuple-element.759), channel_id=1, source_target_pairs={{0,1},{1,2},{2,3},{3,4},{4,5},{5,6},{6,7},{7,8},{8,9},{9,10},{10,1... | collective-permute-start | bytes 73736 | tf_op jit(solution)/shard_map/while/body/eval_jaxpr/ppermute | solution.py:21
  436.1 8.7 %collective-permute-start.5 = (bf16[16,1,768]{2,0,1:T(8,128)(2,1)S(1)}, bf16[16,1,768]{2,0,1:T(8,128)(2,1)S(1)}, u32[]{:S(2)}, u32[]{:S(2)}) collective-permute-start(bf16[16,1,768]{2,0,1:T(8,128)(2,1)S(1)} %get-tuple-element.762), channel_id=1, source_target_pairs={{1,0},{2,1},{3,2},{4,3},{5,4},{6,5},{7,6},{8,7},{9,8},{10,9},{11,1... | collective-permute-start | bytes 73736 | tf_op jit(solution)/shard_map/while/body/eval_jaxpr/ppermute | solution.py:23
  449.1 11.2 %collective-permute-start.7 = (bf16[16,1,768]{2,0,1:T(8,128)(2,1)S(1)}, bf16[16,1,768]{2,0,1:T(8,128)(2,1)S(1)}, u32[]{:S(2)}, u32[]{:S(2)}) collective-permute-start(bf16[16,1,768]{2,0,1:T(8,128)(2,1)S(1)} %get-tuple-element.765), channel_id=1, source_target_pairs={{1,0},{2,1},{3,2},{4,3},{5,4},{6,5},{7,6},{8,7},{9,8},{10,9},{11,1... | collective-permute-start | bytes 73736 | tf_op jit(solution)/shard_map/while/body/eval_jaxpr/ppermute | solution.py:23
  451.1 9.2 %collective-permute-start.8 = (bf16[16,1,768]{2,0,1:T(8,128)(2,1)S(1)}, bf16[16,1,768]{2,0,1:T(8,128)(2,1)S(1)}, u32[]{:S(2)}, u32[]{:S(2)}) collective-permute-start(bf16[16,1,768]{2,0,1:T(8,128)(2,1)S(1)} %get-tuple-element.766), channel_id=1, source_target_pairs={{0,1},{1,2},{2,3},{3,4},{4,5},{5,6},{6,7},{7,8},{8,9},{9,10},{10,1... | collective-permute-start | bytes 73736 | tf_op jit(solution)/shard_map/while/body/eval_jaxpr/ppermute | solution.py:21
  462.4 9.7 %collective-permute-start = (f32[16,8,768]{2,0,1:T(8,128)S(1)}, f32[16,8,768]{2,0,1:T(8,128)S(1)}, u32[]{:S(2)}, u32[]{:S(2)}) collective-permute-start(f32[16,8,768]{2,0,1:T(8,128)S(1)} %broadcast_select_fusion.7), channel_id=1, source_target_pairs={{16,0},{32,16},{48,32},{64,48},{80,64},{96,80},{112,96},{17,1},{33... | collective-permute-start | bytes 1179656 | tf_op jit(solution)/shard_map/while/body/eval_jaxpr/ppermute | solution.py:10
  473.2 9.4 %collective-permute-start.1 = (bf16[16,1,768]{2,0,1:T(8,128)(2,1)S(1)}, bf16[16,1,768]{2,0,1:T(8,128)(2,1)S(1)}, u32[]{:S(2)}, u32[]{:S(2)}) collective-permute-start(bf16[16,1,768]{2,0,1:T(8,128)(2,1)S(1)} %get-tuple-element.754), channel_id=1, source_target_pairs={{1,0},{2,1},{3,2},{4,3},{5,4},{6,5},{7,6},{8,7},{9,8},{10,9},{11,1... | collective-permute-start | bytes 73736 | tf_op jit(solution)/shard_map/while/body/eval_jaxpr/ppermute | solution.py:23
  475.1 8.4 %collective-permute-start.2 = (bf16[16,1,768]{2,0,1:T(8,128)(2,1)S(1)}, bf16[16,1,768]{2,0,1:T(8,128)(2,1)S(1)}, u32[]{:S(2)}, u32[]{:S(2)}) collective-permute-start(bf16[16,1,768]{2,0,1:T(8,128)(2,1)S(1)} %get-tuple-element.755), channel_id=1, source_target_pairs={{0,1},{1,2},{2,3},{3,4},{4,5},{5,6},{6,7},{7,8},{8,9},{9,10},{10,1... | collective-permute-start | bytes 73736 | tf_op jit(solution)/shard_map/while/body/eval_jaxpr/ppermute | solution.py:21
  486.4 14.0 %collective-permute-start.3 = (bf16[16,1,768]{2,0,1:T(8,128)(2,1)S(1)}, bf16[16,1,768]{2,0,1:T(8,128)(2,1)S(1)}, u32[]{:S(2)}, u32[]{:S(2)}) collective-permute-start(bf16[16,1,768]{2,0,1:T(8,128)(2,1)S(1)} %get-tuple-element.758), channel_id=1, source_target_pairs={{1,0},{2,1},{3,2},{4,3},{5,4},{6,5},{7,6},{8,7},{9,8},{10,9},{11,1... | collective-permute-start | bytes 73736 | tf_op jit(solution)/shard_map/while/body/eval_jaxpr/ppermute | solution.py:23
  488.5 11.9 %collective-permute-start.4 = (bf16[16,1,768]{2,0,1:T(8,128)(2,1)S(1)}, bf16[16,1,768]{2,0,1:T(8,128)(2,1)S(1)}, u32[]{:S(2)}, u32[]{:S(2)}) collective-permute-start(bf16[16,1,768]{2,0,1:T(8,128)(2,1)S(1)} %get-tuple-element.759), channel_id=1, source_target_pairs={{0,1},{1,2},{2,3},{3,4},{4,5},{5,6},{6,7},{7,8},{8,9},{9,10},{10,1... | collective-permute-start | bytes 73736 | tf_op jit(solution)/shard_map/while/body/eval_jaxpr/ppermute | solution.py:21
  504.3 8.7 %collective-permute-start.5 = (bf16[16,1,768]{2,0,1:T(8,128)(2,1)S(1)}, bf16[16,1,768]{2,0,1:T(8,128)(2,1)S(1)}, u32[]{:S(2)}, u32[]{:S(2)}) collective-permute-start(bf16[16,1,768]{2,0,1:T(8,128)(2,1)S(1)} %get-tuple-element.762), channel_id=1, source_target_pairs={{1,0},{2,1},{3,2},{4,3},{5,4},{6,5},{7,6},{8,7},{9,8},{10,9},{11,1... | collective-permute-start | bytes 73736 | tf_op jit(solution)/shard_map/while/body/eval_jaxpr/ppermute | solution.py:23
  517.3 11.2 %collective-permute-start.7 = (bf16[16,1,768]{2,0,1:T(8,128)(2,1)S(1)}, bf16[16,1,768]{2,0,1:T(8,128)(2,1)S(1)}, u32[]{:S(2)}, u32[]{:S(2)}) collective-permute-start(bf16[16,1,768]{2,0,1:T(8,128)(2,1)S(1)} %get-tuple-element.765), channel_id=1, source_target_pairs={{1,0},{2,1},{3,2},{4,3},{5,4},{6,5},{7,6},{8,7},{9,8},{10,9},{11,1... | collective-permute-start | bytes 73736 | tf_op jit(solution)/shard_map/while/body/eval_jaxpr/ppermute | solution.py:23
  519.3 9.2 %collective-permute-start.8 = (bf16[16,1,768]{2,0,1:T(8,128)(2,1)S(1)}, bf16[16,1,768]{2,0,1:T(8,128)(2,1)S(1)}, u32[]{:S(2)}, u32[]{:S(2)}) collective-permute-start(bf16[16,1,768]{2,0,1:T(8,128)(2,1)S(1)} %get-tuple-element.766), channel_id=1, source_target_pairs={{0,1},{1,2},{2,3},{3,4},{4,5},{5,6},{6,7},{7,8},{8,9},{9,10},{10,1... | collective-permute-start | bytes 73736 | tf_op jit(solution)/shard_map/while/body/eval_jaxpr/ppermute | solution.py:21
  530.5 9.7 %collective-permute-start = (f32[16,8,768]{2,0,1:T(8,128)S(1)}, f32[16,8,768]{2,0,1:T(8,128)S(1)}, u32[]{:S(2)}, u32[]{:S(2)}) collective-permute-start(f32[16,8,768]{2,0,1:T(8,128)S(1)} %broadcast_select_fusion.7), channel_id=1, source_target_pairs={{16,0},{32,16},{48,32},{64,48},{80,64},{96,80},{112,96},{17,1},{33... | collective-permute-start | bytes 1179656 | tf_op jit(solution)/shard_map/while/body/eval_jaxpr/ppermute | solution.py:10
  541.4 9.4 %collective-permute-start.1 = (bf16[16,1,768]{2,0,1:T(8,128)(2,1)S(1)}, bf16[16,1,768]{2,0,1:T(8,128)(2,1)S(1)}, u32[]{:S(2)}, u32[]{:S(2)}) collective-permute-start(bf16[16,1,768]{2,0,1:T(8,128)(2,1)S(1)} %get-tuple-element.754), channel_id=1, source_target_pairs={{1,0},{2,1},{3,2},{4,3},{5,4},{6,5},{7,6},{8,7},{9,8},{10,9},{11,1... | collective-permute-start | bytes 73736 | tf_op jit(solution)/shard_map/while/body/eval_jaxpr/ppermute | solution.py:23
  543.3 8.4 %collective-permute-start.2 = (bf16[16,1,768]{2,0,1:T(8,128)(2,1)S(1)}, bf16[16,1,768]{2,0,1:T(8,128)(2,1)S(1)}, u32[]{:S(2)}, u32[]{:S(2)}) collective-permute-start(bf16[16,1,768]{2,0,1:T(8,128)(2,1)S(1)} %get-tuple-element.755), channel_id=1, source_target_pairs={{0,1},{1,2},{2,3},{3,4},{4,5},{5,6},{6,7},{7,8},{8,9},{9,10},{10,1... | collective-permute-start | bytes 73736 | tf_op jit(solution)/shard_map/while/body/eval_jaxpr/ppermute | solution.py:21
  554.6 14.0 %collective-permute-start.3 = (bf16[16,1,768]{2,0,1:T(8,128)(2,1)S(1)}, bf16[16,1,768]{2,0,1:T(8,128)(2,1)S(1)}, u32[]{:S(2)}, u32[]{:S(2)}) collective-permute-start(bf16[16,1,768]{2,0,1:T(8,128)(2,1)S(1)} %get-tuple-element.758), channel_id=1, source_target_pairs={{1,0},{2,1},{3,2},{4,3},{5,4},{6,5},{7,6},{8,7},{9,8},{10,9},{11,1... | collective-permute-start | bytes 73736 | tf_op jit(solution)/shard_map/while/body/eval_jaxpr/ppermute | solution.py:23
  556.6 11.9 %collective-permute-start.4 = (bf16[16,1,768]{2,0,1:T(8,128)(2,1)S(1)}, bf16[16,1,768]{2,0,1:T(8,128)(2,1)S(1)}, u32[]{:S(2)}, u32[]{:S(2)}) collective-permute-start(bf16[16,1,768]{2,0,1:T(8,128)(2,1)S(1)} %get-tuple-element.759), channel_id=1, source_target_pairs={{0,1},{1,2},{2,3},{3,4},{4,5},{5,6},{6,7},{7,8},{8,9},{9,10},{10,1... | collective-permute-start | bytes 73736 | tf_op jit(solution)/shard_map/while/body/eval_jaxpr/ppermute | solution.py:21
  572.5 8.7 %collective-permute-start.5 = (bf16[16,1,768]{2,0,1:T(8,128)(2,1)S(1)}, bf16[16,1,768]{2,0,1:T(8,128)(2,1)S(1)}, u32[]{:S(2)}, u32[]{:S(2)}) collective-permute-start(bf16[16,1,768]{2,0,1:T(8,128)(2,1)S(1)} %get-tuple-element.762), channel_id=1, source_target_pairs={{1,0},{2,1},{3,2},{4,3},{5,4},{6,5},{7,6},{8,7},{9,8},{10,9},{11,1... | collective-permute-start | bytes 73736 | tf_op jit(solution)/shard_map/while/body/eval_jaxpr/ppermute | solution.py:23
  585.5 11.2 %collective-permute-start.7 = (bf16[16,1,768]{2,0,1:T(8,128)(2,1)S(1)}, bf16[16,1,768]{2,0,1:T(8,128)(2,1)S(1)}, u32[]{:S(2)}, u32[]{:S(2)}) collective-permute-start(bf16[16,1,768]{2,0,1:T(8,128)(2,1)S(1)} %get-tuple-element.765), channel_id=1, source_target_pairs={{1,0},{2,1},{3,2},{4,3},{5,4},{6,5},{7,6},{8,7},{9,8},{10,9},{11,1... | collective-permute-start | bytes 73736 | tf_op jit(solution)/shard_map/while/body/eval_jaxpr/ppermute | solution.py:23
  587.4 9.2 %collective-permute-start.8 = (bf16[16,1,768]{2,0,1:T(8,128)(2,1)S(1)}, bf16[16,1,768]{2,0,1:T(8,128)(2,1)S(1)}, u32[]{:S(2)}, u32[]{:S(2)}) collective-permute-start(bf16[16,1,768]{2,0,1:T(8,128)(2,1)S(1)} %get-tuple-element.766), channel_id=1, source_target_pairs={{0,1},{1,2},{2,3},{3,4},{4,5},{5,6},{6,7},{7,8},{8,9},{9,10},{10,1... | collective-permute-start | bytes 73736 | tf_op jit(solution)/shard_map/while/body/eval_jaxpr/ppermute | solution.py:21
  (51 other events, 821.2 us)
where the time goes:
time: 683 us; the launch traced here: 679 us
  starting transfers between devices  294 us (43%)
  matrix products  151 us (22%)
  waiting for transfers between devices  80.6 us (12%)
  blocking collectives  78.8 us (12%)
  local copies, waits for them, and re-layouts  48.7 us (7%)
  other arithmetic  20.6 us (3%)
    ppermute x34, starting transfers between devices, with_halo(): lax.ppermute(tail, axis, [(i, (i + 1) % count) for i in range(ends)])  214 us
    psum x1, blocking collectives, on_device(): lax.psum((rec_grad, in_grad, bias_grad, keep_grad, head_grad), ('tm', 'sp...  78.8 us
    dot_general x32, matrix products, run_block(): jnp.einsum('orw,kcrw->okc', dpre, prev_taps[index], preferred_element_typ...  76.3 us
    ppermute x9, waiting for transfers between devices, shifted(): lax.ppermute(value, axis, [(source, source + steps) for source in range(i...  66.7 us
    ppermute x34, starting transfers between devices, with_halo(): lax.ppermute(head, axis, [((i + 1) % count, i) for i in range(ends)])  66.6 us
    dot_general x32, matrix products, run_block(): jnp.einsum('okc,korw->crw', w_rec, back_taps, preferred_element_type=f32)  37.5 us
    dot_general x32, matrix products, run_block(): jnp.einsum('orw,kcrw->okc', dpre, frame_taps[index], preferred_element_ty...  20.5 us
    while x240, local copies, waits for them, and re-layouts  19.5 us
  transfers between devices with their start and end apart: 77, of which 25 were waited for; matrix products, arithmetic and copies ran while one was open for 15% of the time, Pallas kernels for 0%

commit v1 on v0

v1 whole, which is shorter than its diff:
```python
import functools

import jax
import jax.numpy as jnp
from jax import lax
from jax.experimental import pallas as pl
from jax.experimental.pallas import tpu as pltpu
from jax.sharding import PartitionSpec as P

MESH = pl.DeviceIdType.MESH
F32 = jnp.float32
BF16 = jnp.bfloat16
W = 128
CH = 16
ROWS = 8
STEPS = 4
HALO = [STEPS + 1 - k for k in range(STEPS)]
A_AT = [0, 5, 9]
B_AT = [12, 17, 21, 24]
MSG = 26 * CH
TILE = ROWS * CH


def dot(a, b):
    return lax.dot_general(a, b, (((1,), (0,)), ((), ())), preferred_element_type=F32)


def dot_exact(a, b):
    return lax.dot_general(a, b, (((1,), (0,)), ((), ())), preferred_element_type=F32, precision=lax.Precision.HIGHEST)


def dot_nt(a, b):
    return lax.dot_general(a, b, (((1,), (1,)), ((), ())), preferred_element_type=F32)


def iota2(shape, dim):
    return lax.broadcasted_iota(jnp.int32, shape, dim)


def onehot(cond):
    return jnp.where(cond, 1.0, 0.0).astype(BF16)


def tiles(value, count):
    return [value[CH * i : CH * (i + 1)] for i in range(count)]


def kernel(
    tm_count, space_count, cols, chunks,
    frames_ref, states_ref, start_ref, cot_ref, small_ref, chan_ref,
    gf_ref, bound_ref, sums_ref,
    zpa, zpb, za, zb, qsend, stage_up, stage_dn, h_up, h_dn, p_up, p_dn, p_stage_up, p_stage_dn,
    slopes, pushed, xs, dkeep, gkeep, gfs, bnd, c_own, c_up, c_dn, c_send,
    wa, wb, wp, wt, d1prev, d2prev, gprev, biasb, retb, gram, headacc, rpart, rs, ag, red,
    h_ssem, h_rsem, p_ssem, p_rsem, e_ssem, c_ssem, c_rsem, s1, r1, s2, r2, s3, r3,
):
    tm = lax.axis_index("tm")
    sp = lax.axis_index("space")
    has_up = sp > 0
    has_dn = sp < space_count - 1
    is_last = tm == tm_count - 1
    is_first = tm == 0
    blocks = cols // W
    skew0 = STEPS * (tm_count - 1 - tm)

    zh = jnp.zeros((MSG, W), BF16)
    z2 = jnp.zeros((2 * CH, W), BF16)
    h_up[0] = zh
    h_dn[0] = zh
    p_up[0] = z2
    p_dn[0] = z2
    for k in range(STEPS):
        za[0, k] = jnp.zeros((TILE, W), BF16)
        zb[0, k] = jnp.zeros((TILE, W), BF16)
        gprev[k] = jnp.zeros((16 * CH, W), F32)
        d1prev[k] = jnp.zeros((16 * CH, W), BF16)
        d2prev[k] = jnp.zeros((16 * CH, W), BF16)
    gram[...] = jnp.zeros_like(gram)

    @pl.when(jnp.logical_not(has_up))
    def _():
        for j in range(chunks):
            h_up[j + 1] = zh
            p_up[j + 1] = z2
            c_up[j] = jnp.zeros((STEPS * CH, W), BF16)

    @pl.when(jnp.logical_not(has_dn))
    def _():
        for j in range(chunks):
            h_dn[j + 1] = zh
            p_dn[j + 1] = z2
            c_dn[j] = jnp.zeros((STEPS * CH, W), BF16)

    @pl.when(is_last)
    def _():
        for j in range(chunks):
            c_own[j] = jnp.zeros((TILE, W), BF16)
            c_up[j] = jnp.zeros((STEPS * CH, W), BF16)
            c_dn[j] = jnp.zeros((STEPS * CH, W), BF16)

    barrier = pltpu.get_barrier_semaphore()

    def greet(t, s):
        pl.semaphore_signal(barrier, inc=1, device_id=(t, s), device_id_type=MESH)

    for p in range(1, tm_count):
        greet(lax.rem(tm + p, tm_count), sp)
    for q in range(1, space_count):
        greet(tm, lax.rem(sp + q, space_count))
    for dt in (1, tm_count - 1):
        for ds in (1, space_count - 1):
            greet(lax.rem(tm + dt, tm_count), lax.rem(sp + ds, space_count))

    pr = iota2((TILE, TILE), 0)
    pc = iota2((TILE, TILE), 1)
    perm_a = onehot((pr // CH == lax.rem(pc, ROWS)) & (lax.rem(pr, CH) == pc // ROWS))
    bc = iota2((TILE, 15 * ROWS), 1)
    br = iota2((TILE, 15 * ROWS), 0)
    b_chan = bc // ROWS
    b_chan = b_chan + jnp.where(b_chan >= 3, 1, 0)
    perm_b = onehot((br // CH == lax.rem(bc, ROWS)) & (lax.rem(br, CH) == b_chan))
    ones_b = jnp.where(lax.rem(iota2((TILE, cols), 0), CH) == 3, 1.0, 0.0)

    def flat(value, channels):
        return value.astype(F32).reshape(channels * ROWS, cols)

    def put(ref, index, value):
        value = value.astype(BF16)
        ref[index, 0] = jnp.zeros((TILE, W), BF16)
        for c in range(blocks):
            ref[index, c + 1] = value[:, W * c : W * (c + 1)]
        for c in range(blocks + 1, chunks + 1):
            ref[index, c] = jnp.zeros((TILE, W), BF16)

    for f in range(STEPS):
        put(zpa, f, dot(perm_a, flat(states_ref[f], CH).astype(BF16)))
        both = jnp.concatenate([flat(frames_ref[f], 3), flat(cot_ref[f], 12)], axis=0).astype(BF16)
        put(zpb, f, dot(perm_b, both) + ones_b)

    @pl.when(is_first)
    def _():
        put(zpa, STEPS, dot(perm_a, flat(start_ref[...], CH).astype(BF16)))

    pl.semaphore_wait(barrier, tm_count - 1 + space_count - 1 + 4)

    def h_copy(j, up):
        src, dst, target = (stage_up, h_dn, sp - 1) if up else (stage_dn, h_up, sp + 1)
        way = 0 if up else 1
        return pltpu.make_async_remote_copy(
            src_ref=src.at[j], dst_ref=dst.at[j + 1], send_sem=h_ssem.at[way, j], recv_sem=h_rsem.at[way, j],
            device_id=(tm, target), device_id_type=MESH,
        )

    def p_copy(j, way):
        src = [qsend.at[j], qsend.at[j, pl.ds(0, 2 * CH)], qsend.at[j, pl.ds(6 * CH, 2 * CH)]][way]
        dst = [za.at[j + 1, STEPS - 1], p_dn.at[j + 1], p_up.at[j + 1]][way]
        target = (tm + 1, [sp, sp - 1, sp + 1][way])
        return pltpu.make_async_remote_copy(
            src_ref=src, dst_ref=dst, send_sem=p_ssem.at[way, j], recv_sem=p_rsem.at[way, j],
            device_id=target, device_id_type=MESH,
        )

    def s_copy(j, way):
        src = [None, p_stage_up.at[j], p_stage_dn.at[j]][way]
        dst = [None, p_dn.at[j + 1], p_up.at[j + 1]][way]
        target = (tm, [sp, sp - 1, sp + 1][way])
        return pltpu.make_async_remote_copy(
            src_ref=src, dst_ref=dst, send_sem=e_ssem.at[way, j], recv_sem=p_rsem.at[way, j],
            device_id=target, device_id_type=MESH,
        )

    def c_copy(j, way):
        src = [c_send.at[j], c_send.at[j, pl.ds(0, STEPS * CH)], c_send.at[j, pl.ds(STEPS * CH, STEPS * CH)]][way]
        dst = [c_own.at[j], c_dn.at[j], c_up.at[j]][way]
        target = (tm - 1, [sp, sp - 1, sp + 1][way])
        return pltpu.make_async_remote_copy(
            src_ref=src, dst_ref=dst, send_sem=c_ssem.at[way, j], recv_sem=c_rsem.at[way, j],
            device_id=target, device_id_type=MESH,
        )

    def skewer(shift):
        return onehot(iota2((2 * W, W), 0) == iota2((2 * W, W), 1) + (W - shift))

    def skewed(ref, index, j, shift):
        wide = jnp.concatenate([ref[index, j], ref[index, j + 1]], axis=1)
        return dot(wide, skewer(shift)).astype(BF16)

    def send_chunk(j, carry):
        for k in range(STEPS):
            h = HALO[k]
            b_val = skewed(zpb, STEPS - 1 - k, j, skew0 + k)
            zb[j + 1, k] = b_val
            stage_up[j, B_AT[k] * CH : (B_AT[k] + h) * CH] = b_val[: h * CH]
            stage_dn[j, B_AT[k] * CH : (B_AT[k] + h) * CH] = b_val[TILE - h * CH :]
            if k < STEPS - 1:
                a_val = skewed(zpa, STEPS - 2 - k, j, skew0 + k)
                za[j + 1, k] = a_val
                stage_up[j, A_AT[k] * CH : (A_AT[k] + h) * CH] = a_val[: h * CH]
                stage_dn[j, A_AT[k] * CH : (A_AT[k] + h) * CH] = a_val[TILE - h * CH :]

        @pl.when(has_up)
        def _():
            h_copy(j, True).start()

        @pl.when(has_dn)
        def _():
            h_copy(j, False).start()

        @pl.when(jnp.logical_not(is_last))
        def _():
            qsend[j] = skewed(zpa, STEPS - 1, j, skew0 - 1)
            p_copy(j, 0).start()

            @pl.when(has_up)
            def _():
                p_copy(j, 1).start()

            @pl.when(has_dn)
            def _():
                p_copy(j, 2).start()

        @pl.when(is_first)
        def _():
            a_val = skewed(zpa, STEPS, j, skew0 + STEPS - 1)
            za[j + 1, STEPS - 1] = a_val
            p_stage_up[j] = a_val[: 2 * CH]
            p_stage_dn[j] = a_val[6 * CH :]

            @pl.when(has_up)
            def _():
                s_copy(j, 1).start()

            @pl.when(has_dn)
            def _():
                s_copy(j, 2).start()

        return carry

    lax.fori_loop(0, chunks, send_chunk, 0)

    small = small_ref[...]
    biasb[...] = jnp.concatenate([jnp.broadcast_to(chan_ref[:, 0:1], (CH, W))] * 16, axis=0)
    retb[...] = jnp.concatenate([jnp.broadcast_to(chan_ref[:, 1:2], (CH, W))] * 16, axis=0)

    def spread(rows, cols_n, flat_w, width, pick, at, relation):
        r_i = iota2((rows, cols_n), 0) // CH
        c_i = iota2((rows, cols_n), 1) // CH
        left = onehot(lax.rem(iota2((rows, CH), 0), CH) == iota2((rows, CH), 1))
        base = dot(left, flat_w).astype(BF16)
        total = jnp.zeros((rows, cols_n), F32)
        s_r = iota2((width, cols_n), 0)
        s_c = lax.rem(iota2((width, cols_n), 1), CH)
        for a in range(3):
            part = dot(base, onehot(pick(a, s_r, s_c)))
            total = jnp.where(relation(r_i, c_i) == a, part, total)
        return total.astype(BF16)

    fwd = small[:, 0:144]
    bwd = small[:, 144:288]
    fwd_in = small[:, 288:320]
    head_t = small[:, 320:336]
    bwd_in = small[:, 336:480]
    for m in range(3):
        b = 2 - m
        ahead = lambda r, c: c - r
        wa[m] = spread(256, 288, fwd, 144, lambda a, s, c: s == (3 * a + b) * CH + c, 0, ahead)
        wb[m] = spread(256, 288, fwd_in, 32, lambda a, s, c: (s == (3 * a + b) * 3 + c) & (c < 3), 0, ahead)
    wp[...] = spread(256, 288, head_t, 16, lambda a, s, c: (s == c - 4) & (c >= 4) & (a == 1), 0, ahead)
    for b in range(3):
        behind = lambda r, c: r + 2 - c
        t_b = spread(224, 256, bwd, 144, lambda a, s, c: s == (3 * a + b) * CH + c, 0, behind)
        rr = iota2((32, 256), 0)
        left = onehot(rr[:, :CH] // ROWS == iota2((32, CH), 1))
        base = dot(left, bwd_in).astype(BF16)
        for k in range(STEPS):
            n = 16 - 2 * k
            first = STEPS - 1 - k
            r_i = lax.rem(rr, ROWS)
            c_i = iota2((32, 256), 1) // CH - first
            total = jnp.zeros((32, 256), F32)
            for a in range(3):
                s_r = iota2((144, 256), 0)
                s_c = lax.rem(iota2((144, 256), 1), CH)
                part = dot(base, onehot(s_r == (3 * a + b) * CH + s_c))
                total = jnp.where(r_i + 2 - c_i == a, part, total)
            wt[k, b, 0 : CH * (n - 2)] = t_b[0 : CH * (n - 2)]
            wt[k, b, CH * (n - 2) : CH * n] = total.astype(BF16)

    lane = iota2((1, W), 1)

    def shifted(now, before, steps):
        moved = pltpu.roll(now, steps, 1)
        return moved, jnp.where(lane >= steps, moved, before)

    def get_slopes(j):
        for k in range(STEPS):
            h = HALO[k]
            n = 16 - 2 * k

            def whole(slot):
                if k < STEPS - 1:
                    up_a = h_up[slot, A_AT[k] * CH : (A_AT[k] + h) * CH]
                    dn_a = h_dn[slot, A_AT[k] * CH : (A_AT[k] + h) * CH]
                else:
                    up_a, dn_a = p_up[slot], p_dn[slot]
                up_b = h_up[slot, B_AT[k] * CH : (B_AT[k] + h) * CH]
                dn_b = h_dn[slot, B_AT[k] * CH : (B_AT[k] + h) * CH]
                return (
                    jnp.concatenate([up_a, za[slot, k], dn_a], axis=0),
                    jnp.concatenate([up_b, zb[slot, k], dn_b], axis=0),
                )

            a_now, b_now = whole(j + 1)
            a_old, b_old = whole(j)
            both = jnp.concatenate([a_now, b_now], axis=0)
            both_old = jnp.concatenate([a_old, b_old], axis=0)
            size = CH * (n + 2)
            preact = biasb[0 : CH * n]
            for m in range(3):
                if m == 0:
                    x = both
                else:
                    x = jnp.where(lane >= m, pltpu.roll(both, m, 1), pltpu.roll(both_old, m, 1))
                x_a, x_b = x[:size], x[size:]
                preact = preact + dot(wa[m, 0 : CH * n, 0:size], x_a) + dot(wb[m, 0 : CH * n, 0:size], x_b)
                if m == 1:
                    pushed[j, k, 0 : CH * n] = dot(wp[0 : CH * n, 0:size], x_b)
                low = (h - 1) * CH
                xs[j, k, m, 0 : 10 * CH] = x_a[low : low + 10 * CH]
                xs[j, k, m, 10 * CH : 20 * CH] = x_b[low : low + 10 * CH]
            col = W * j + lane - (skew0 + k + 1)
            row = ROWS * sp + iota2((CH * n, 1), 0) // CH + (k - STEPS)
            inside = (col >= 0) & (col < cols) & (row >= 0) & (row < ROWS * space_count)
            t = jnp.tanh(preact)
            slopes[j, k, 0 : CH * n] = jnp.where(inside, 1.0 - t * t, 0.0)

    def await_inputs(j):
        @pl.when(has_up)
        def _():
            h_copy(j, False).wait_recv()

        @pl.when(has_dn)
        def _():
            h_copy(j, True).wait_recv()

        @pl.when(jnp.logical_not(is_first))
        def _():
            p_copy(j, 0).wait_recv()

        @pl.when(has_dn)
        def _():
            p_copy(j, 1).wait_recv()

        @pl.when(has_up)
        def _():
            p_copy(j, 2).wait_recv()

    def prepare(j, carry):
        await_inputs(j)
        get_slopes(j)
        return carry

    def post(j, carry):
        for k in range(STEPS):
            zero = jnp.zeros((CH, W), BF16)
            d = tiles(dkeep[j, k], ROWS)
            g = tiles(gkeep[j, k], ROWS)
            right = jnp.concatenate(
                [
                    jnp.concatenate(d + [zero, zero], axis=1),
                    jnp.concatenate([zero] + d + [zero], axis=1),
                    jnp.concatenate([zero, zero] + d, axis=1),
                    jnp.concatenate([zero] + g + [zero], axis=1),
                ],
                axis=0,
            )
            rows_of = []
            for half in range(2):
                for m in range(3):
                    x = xs[j, k, m, half * 10 * CH : (half + 1) * 10 * CH]
                    rows_of.append(jnp.concatenate(tiles(x, 10), axis=1))
            left = jnp.concatenate(rows_of, axis=0)
            gram[...] += dot_nt(left, right)
        return carry

    def chain(j):
        carried = jnp.concatenate([c_up[j], c_own[j], c_dn[j]], axis=0).astype(F32)
        for k in range(STEPS):
            n = 16 - 2 * k
            size = CH * n
            g = carried + pushed[j, k, 0:size]
            d = (g * slopes[j, k, 0:size]).astype(BF16)
            r1_, d1 = shifted(d, d1prev[k, 0:size], 1)
            r2_, d2 = shifted(d, d2prev[k, 0:size], 2)
            d1prev[k, 0:size] = r1_
            d2prev[k, 0:size] = r2_
            inner = g[CH : size - CH]
            rg, gs = shifted(inner, gprev[k, 0 : size - 2 * CH], 1)
            gprev[k, 0 : size - 2 * CH] = rg
            conv = (
                dot(wt[k, 0, 0:size, 0:size], d)
                + dot(wt[k, 1, 0:size, 0:size], d1)
                + dot(wt[k, 2, 0:size, 0:size], d2)
            )
            carried = retb[0 : size - 2 * CH] * gs + conv[0 : size - 2 * CH]
            gfs[j, k] = conv[size - 2 * CH : size]
            at = (STEPS - k) * CH
            dkeep[j, k] = d[at : at + TILE]
            gkeep[j, k] = g[at : at + TILE].astype(BF16)
        bnd[j] = carried
        c_send[j] = carried.astype(BF16)

    def step(j, carry):
        @pl.when(is_last)
        def _():
            prepare(j, 0)

        @pl.when(jnp.logical_not(is_last))
        def _():
            c_copy(j, 0).wait_recv()

            @pl.when(has_dn)
            def _():
                c_copy(j, 1).wait_recv()

            @pl.when(has_up)
            def _():
                c_copy(j, 2).wait_recv()

        chain(j)

        @pl.when(jnp.logical_not(is_first))
        def _():
            c_copy(j, 0).start()

            @pl.when(has_up)
            def _():
                c_copy(j, 1).start()

            @pl.when(has_dn)
            def _():
                c_copy(j, 2).start()

        @pl.when(jnp.logical_not(is_last))
        def _():
            post(j, 0)

        return carry

    @pl.when(jnp.logical_not(is_last))
    def _():
        lax.fori_loop(0, chunks, prepare, 0)

    total = jnp.zeros((12 * ROWS, TILE), F32)
    for f in range(STEPS):
        total = total + dot_nt(flat(cot_ref[f], 12).astype(BF16), flat(states_ref[f], CH).astype(BF16))
    same = lax.rem(iota2((12 * ROWS, TILE), 0), ROWS) == lax.rem(iota2((12 * ROWS, TILE), 1), ROWS)
    total = jnp.where(same, total, 0.0)
    pick_l = jnp.where(iota2((CH, 12 * ROWS), 0) == iota2((CH, 12 * ROWS), 1) // ROWS, 1.0, 0.0)
    pick_r = jnp.where(iota2((TILE, W), 0) // ROWS == iota2((TILE, W), 1), 1.0, 0.0)
    headacc[...] = dot_exact(dot_exact(pick_l, total), pick_r)

    lax.fori_loop(0, chunks, step, 0)

    @pl.when(is_last)
    def _():
        lax.fori_loop(0, chunks, post, 0)

    rpart[0:48, 0:64] = gram[0:48]
    rpart[0:48, 64:128] = gram[48:96]
    rpart[48:64] = headacc[...]
    piece = 64 // tm_count

    def cut(t):
        return pl.ds(pl.multiple_of(t * piece, 8), piece)

    def first_copy(p):
        t = lax.rem(tm + p, tm_count)
        return pltpu.make_async_remote_copy(
            src_ref=rpart.at[cut(t)], dst_ref=rs.at[p], send_sem=s1.at[p], recv_sem=r1.at[p],
            device_id=(t, sp), device_id_type=MESH,
        )

    for p in range(1, tm_count):
        first_copy(p).start()

    out_shift = skew0 + STEPS + 1
    for c in range(blocks):
        def unskew(now, after, shift):
            return jnp.where(lane < W - shift, pltpu.roll(now, W - shift, 1), pltpu.roll(after, W - shift, 1))

        value = unskew(bnd[c], bnd[c + 1], out_shift)
        for r in range(ROWS):
            bound_ref[r, :, W * c : W * (c + 1)] = value[CH * r : CH * (r + 1)]
        for k in range(STEPS):
            value = unskew(gfs[c, k, 0:24], gfs[c + 1, k, 0:24], skew0 + k + 2)
            gf_ref[STEPS - 1 - k, :, :, W * c : W * (c + 1)] = value.reshape(3, ROWS, W).astype(BF16)

    part = rpart[cut(tm)]
    for p in range(1, tm_count):
        first_copy(p).wait_recv()
        part = part + rs[p]
    ag[sp] = part

    def second_copy(q):
        s = lax.rem(sp + q, space_count)
        return pltpu.make_async_remote_copy(
            src_ref=ag.at[sp], dst_ref=ag.at[sp], send_sem=s2.at[q], recv_sem=r2.at[q],
            device_id=(tm, s), device_id_type=MESH,
        )

    for q in range(1, space_count):
        second_copy(q).start()
    for q in range(1, space_count):
        second_copy(q).wait_recv()
    part = ag[0]
    for q in range(1, space_count):
        part = part + ag[q]
    red[cut(tm)] = part

    def third_copy(p):
        t = lax.rem(tm + p, tm_count)
        return pltpu.make_async_remote_copy(
            src_ref=red.at[cut(tm)], dst_ref=red.at[cut(tm)], send_sem=s3.at[p], recv_sem=r3.at[p],
            device_id=(t, sp), device_id_type=MESH,
        )

    for p in range(1, tm_count):
        third_copy(p).start()
    for p in range(1, tm_count):
        third_copy(p).wait_recv()
    sums_ref[...] = red[...]

    for p in range(1, tm_count):
        first_copy(p).wait_send()
        third_copy(p).wait_send()
    for q in range(1, space_count):
        second_copy(q).wait_send()

    def drain(j, carry):
        @pl.when(has_up)
        def _():
            h_copy(j, True).wait_send()

        @pl.when(has_dn)
        def _():
            h_copy(j, False).wait_send()

        @pl.when(jnp.logical_not(is_last))
        def _():
            p_copy(j, 0).wait_send()

            @pl.when(has_up)
            def _():
                p_copy(j, 1).wait_send()

            @pl.when(has_dn)
            def _():
                p_copy(j, 2).wait_send()

        @pl.when(is_first)
        def _():
            @pl.when(has_up)
            def _():
                s_copy(j, 1).wait_send()

            @pl.when(has_dn)
            def _():
                s_copy(j, 2).wait_send()

        @pl.when(jnp.logical_not(is_first))
        def _():
            c_copy(j, 0).wait_send()

            @pl.when(has_up)
            def _():
                c_copy(j, 1).wait_send()

            @pl.when(has_dn)
            def _():
                c_copy(j, 2).wait_send()

        return carry

    lax.fori_loop(0, chunks, drain, 0)


def on_device(tm_count, space_count, frames, states, start_state, cotangent, w_rec, w_in, bias_vec, retain, w_head):
    cols = states.shape[3]
    chunks = -(-(cols + STEPS * tm_count + 1) // W)
    pad = lambda value, rows, width: jnp.pad(value, ((0, rows - value.shape[0]), (0, width - value.shape[1])))
    small = jnp.concatenate(
        [
            w_rec.reshape(16, 144),
            w_rec.transpose(2, 1, 0).reshape(16, 144),
            pad(w_in.reshape(16, 27), 16, 32),
            pad(w_head.T, 16, 16),
            pad(w_in.transpose(2, 1, 0).reshape(3, 144), 16, 144),
        ],
        axis=1,
    )
    small = pad(small, 16, 512)
    chan = jnp.stack([bias_vec, retain], axis=1)
    vmem = pl.BlockSpec(memory_space=pltpu.VMEM)
    dma = pltpu.SemaphoreType.DMA
    scratch = [
        pltpu.VMEM((STEPS + 1, chunks + 1, TILE, W), BF16),
        pltpu.VMEM((STEPS, chunks + 1, TILE, W), BF16),
        pltpu.VMEM((chunks + 1, STEPS, TILE, W), BF16),
        pltpu.VMEM((chunks + 1, STEPS, TILE, W), BF16),
        pltpu.VMEM((chunks, TILE, W), BF16),
        pltpu.VMEM((chunks, MSG, W), BF16),
        pltpu.VMEM((chunks, MSG, W), BF16),
        pltpu.VMEM((chunks + 1, MSG, W), BF16),
        pltpu.VMEM((chunks + 1, MSG, W), BF16),
        pltpu.VMEM((chunks + 1, 2 * CH, W), BF16),
        pltpu.VMEM((chunks + 1, 2 * CH, W), BF16),
        pltpu.VMEM((chunks, 2 * CH, W), BF16),
        pltpu.VMEM((chunks, 2 * CH, W), BF16),
        pltpu.VMEM((chunks, STEPS, 256, W), F32),
        pltpu.VMEM((chunks, STEPS, 256, W), F32),
        pltpu.VMEM((chunks, STEPS, 3, 20 * CH, W), BF16),
        pltpu.VMEM((chunks, STEPS, TILE, W), BF16),
        pltpu.VMEM((chunks, STEPS, TILE, W), BF16),
        pltpu.VMEM((chunks, STEPS, 32, W), F32),
        pltpu.VMEM((chunks, TILE, W), F32),
        pltpu.VMEM((chunks, TILE, W), BF16),
        pltpu.VMEM((chunks, STEPS * CH, W), BF16),
        pltpu.VMEM((chunks, STEPS * CH, W), BF16),
        pltpu.VMEM((chunks, TILE, W), BF16),
        pltpu.VMEM((3, 256, 288), BF16),
        pltpu.VMEM((3, 256, 288), BF16),
        pltpu.VMEM((256, 288), BF16),
        pltpu.VMEM((STEPS, 3, 256, 256), BF16),
        pltpu.VMEM((STEPS, 256, W), BF16),
        pltpu.VMEM((STEPS, 256, W), BF16),
        pltpu.VMEM((STEPS, 256, W), F32),
        pltpu.VMEM((256, W), F32),
        pltpu.VMEM((256, W), F32),
        pltpu.VMEM((96, 64), F32),
        pltpu.VMEM((CH, W), F32),
        pltpu.VMEM((64, W), F32),
        pltpu.VMEM((tm_count, 64 // tm_count, W), F32),
        pltpu.VMEM((space_count, 64 // tm_count, W), F32),
        pltpu.VMEM((64, W), F32),
        dma((2, chunks)), dma((2, chunks)),
        dma((3, chunks)), dma((3, chunks)), dma((3, chunks)),
        dma((3, chunks)), dma((3, chunks)),
        dma((tm_count,)), dma((tm_count,)),
        dma((space_count,)), dma((space_count,)),
        dma((tm_count,)), dma((tm_count,)),
    ]
    grad_frames, bound, sums = pl.pallas_call(
        functools.partial(kernel, tm_count, space_count, cols, chunks),
        out_shape=[
            jax.ShapeDtypeStruct((STEPS, 3, ROWS, cols), BF16),
            jax.ShapeDtypeStruct((ROWS, CH, cols), F32),
            jax.ShapeDtypeStruct((64, W), F32),
        ],
        in_specs=[vmem] * 6,
        out_specs=[vmem] * 3,
        scratch_shapes=scratch,
        compiler_params=pltpu.CompilerParams(
            collective_id=0, has_side_effects=True, vmem_limit_bytes=56 * 1024 * 1024
        ),
    )(frames, states, start_state, cotangent, small, chan)
    def taps(block, width):
        parts = block[:, :, 0:48].reshape(3, CH, 3, CH)[::-1, :width]
        return parts.transpose(3, 2, 0, 1).reshape(CH, 9, width)

    rec = sums[0:48, 0:64].reshape(3, CH, 64)
    other = sums[0:48, 64:128].reshape(3, CH, 64)
    grad_rec = taps(rec, CH)
    grad_in = taps(other, 3)
    grad_bias = other[1, 3, 16:32]
    eye = jnp.eye(CH, dtype=bool)
    grad_retain = jnp.sum(jnp.where(eye, rec[1, :, 48:64], 0.0), axis=0)
    grad_head = sums[48:60, 0:16]
    return (grad_rec, grad_in, grad_bias, grad_retain, grad_head, grad_frames, bound.transpose(1, 0, 2)[None])


def solution(mesh):
    banded = P("tm", None, "space", None)
    in_specs = (banded, banded, P(None, "space", None), banded, P(), P(), P(), P(), P())
    out_specs = (P(), P(), P(), P(), P(), banded, banded)
    return jax.shard_map(
        functools.partial(on_device, mesh.shape["tm"], mesh.shape["space"]),
        mesh=mesh, in_specs=in_specs, out_specs=out_specs, check_vma=False,
    )
```

time: 683 us -> 104 us (0.15)
  starting transfers between devices: 294 us -> 0 us
  matrix products: 151 us -> 0 us
  Pallas kernels: 0 us -> 92.8 us
  waiting for transfers between devices: 80.6 us -> 0 us
  blocking collectives: 78.8 us -> 0 us
  local copies, waits for them, and re-layouts: 48.7 us -> 8.87 us
  other arithmetic: 20.6 us -> 1.29 us
    ppermute x77 -> x0, starting transfers between devices: 294 us -> none  [the longest x34 214 us: with_halo(): lax.ppermute(tail, axis, [(i, (i + 1) % count) for i in range(ends)])]
    dot_general x132 -> x0, matrix products: 151 us -> none  [the longest x32 76.3 us: run_block(): jnp.einsum('orw,kcrw->okc', dpre, prev_taps[index], preferred_element_typ...]
    pallas_call x0 -> x1, Pallas kernels: none -> 92.8 us  [on_device(): pl.pallas_call(functools.partial(kernel, tm_count, space_count, cols, chu...]
    ppermute x77 -> x0, waiting for transfers between devices: 80.6 us -> none  [the longest x9 66.7 us: shifted(): lax.ppermute(value, axis, [(source, source + steps) for source in range(i...]
    psum x1 -> x0, blocking collectives: 78.8 us -> none  [on_device(): lax.psum((rec_grad, in_grad, bias_grad, keep_grad, head_grad), ('tm', 'sp...]
    while x243 -> x0, local copies, waits for them, and re-layouts: 21.2 us -> none
    another operation x44 -> x1, local copies, waits for them, and re-layouts: 15.8 us -> 0.68 us  [on_device(): chan = jnp.stack([bias_vec, retain], axis=1)]
    reduce_sum x8 -> x1, other arithmetic: 9.44 us -> 0.6 us  [on_device(): grad_retain = jnp.sum(jnp.where(eye, rec[1, :, 48:64], 0.0), axis=0)]
  transfers between devices with their start and end apart: 77 -> 0, of which waited for: 25 -> 0; matrix products, arithmetic and copies ran while one was open for 15% -> 0% of each run, Pallas kernels for 0% -> 0%
where the time goes in v1:
time: 104 us
  Pallas kernels  92.8 us (89%)
  local copies, waits for them, and re-layouts  8.87 us (9%)
  other arithmetic  1.29 us (1%)
    pallas_call x1, Pallas kernels, on_device(): pl.pallas_call(functools.partial(kernel, tm_count, space_count, cols, chu...  92.8 us
    unnamed x12, local copies, waits for them, and re-layouts  4.3 us

profile of v1, /device:TPU:1, one launch (start us, length us, event | category | flops | bytes accessed | tf_op | source)
XLA Modules:
  0.0 103.7 jit_solution(3071441175960806292)
XLA Ops:
  0.6 0.0 copy-start.1
  0.6 0.7 pad_maximum_fusion
  1.3 0.8 copy.48
  2.1 0.7 copy.52.chan_ref
  2.8 0.0 copy-done.1
  2.8 0.0 copy-start.3
  2.8 0.1 copy.51
  2.9 0.6 copy-done.3
  3.5 0.1 copy.47
  3.6 0.1 reshape.47
  3.7 0.1 copy.46
  3.8 0.1 copy.50
  3.9 0.1 concatenate.3
  4.0 0.6 pad.19.small_ref
  4.6 92.8 %shard_map.144 = (bf16[4,3,8,768]{3,2,1,0:T(8,128)(2,1)}, f32[8,16,768]{2,1,0:T(8,128)}, f32[64,128]{1,0:T(8,128)}) custom-call(bf16[4,3,8,768]{3,2,1,0:T(8,128)(2,1)} %frames_ref.1, bf16[4,16,8,768]{3,2,1,0:T(8,128)(2,1)} %states_ref.1, bf16[16,8,768]{2,1,0:T(8,128)(2,1)} %start_ref.1, bf16[4,12,8,768]{3,2,1,0:T(8,128)(2,1)} %cot_ref.1, ...), custom_call_target="tpu_custom_call" | custom-call | tf_op jit(solution)/shard_map/pallas_call | solution.py:653
  97.4 0.0 copy-start.2
  97.5 2.0 %copy.55 = f32[1,16,8,768]{3,2,1,0:T(8,128)} copy(f32[1,16,8,768]{3,1,2,0:T(8,128)} %bitcast.31) | data formatting | bytes 786432
  99.4 0.0 copy-done.2
  99.4 0.6 slice.31
  100.0 0.1 fusion.2
  100.1 0.6 fusion.1
  100.7 0.6 slice_bitcast_fusion.1
  101.3 0.1 reshape.52
  101.4 0.6 copy.54
  102.0 0.1 reshape.49
  102.1 0.0 copy-start
  102.2 0.7 copy.53
  102.9 0.1 copy-done
  103.0 0.7 copy.57
  (8 shorter events, 0.1 us)
Async XLA Ops:
  0.6 2.2 %copy-start.1 = (bf16[16,9,16]{2,0,1:T(8,128)(2,1)S(1)}, bf16[16,9,16]{2,0,1:T(8,128)(2,1)}, u32[]{:S(2)}) copy-start(bf16[16,9,16]{2,0,1:T(8,128)(2,1)} %param.13) | copy-start | bytes 13828
  2.8 0.7 copy-start.3
  97.4 2.0 %copy-start.2 = (f32[64,128]{1,0:T(8,128)S(1)}, f32[64,128]{1,0:T(8,128)}, u32[]{:S(2)}) copy-start(f32[64,128]{1,0:T(8,128)} %get-tuple-element.10) | copy-start | bytes 98308
  102.1 0.9 copy-start

commit v2 on v1

--- a/solution.py
+++ b/solution.py
@@ -29,6 +29,10 @@
     return lax.dot_general(a, b, (((1,), (0,)), ((), ())), preferred_element_type=F32, precision=lax.Precision.HIGHEST)
 
 
+def dot_tn(a, b):
+    return lax.dot_general(a, b, (((0,), (0,)), ((), ())), preferred_element_type=F32)
+
+
 def dot_nt(a, b):
     return lax.dot_general(a, b, (((1,), (1,)), ((), ())), preferred_element_type=F32)
 
@@ -47,12 +51,13 @@
 
 def kernel(
     tm_count, space_count, cols, chunks,
-    frames_ref, states_ref, start_ref, cot_ref, small_ref, chan_ref,
+    frames_in, states_in, start_in, cot_in, wrec_ref, win_ref, bias_ref, retain_ref, whead_ref,
     gf_ref, bound_ref, sums_ref,
+    frames_ref, states_ref, start_ref, cot_ref,
     zpa, zpb, za, zb, qsend, stage_up, stage_dn, h_up, h_dn, p_up, p_dn, p_stage_up, p_stage_dn,
     slopes, pushed, xs, dkeep, gkeep, gfs, bnd, c_own, c_up, c_dn, c_send,
-    wa, wb, wp, wt, d1prev, d2prev, gprev, biasb, retb, gram, headacc, rpart, rs, ag, red,
-    h_ssem, h_rsem, p_ssem, p_rsem, e_ssem, c_ssem, c_rsem, s1, r1, s2, r2, s3, r3,
+    wf0, wf1, wf2, wf3, wp, wt0, wt1, wt2, wt3, d1prev, d2prev, gprev, biasb, retb, gram, headacc, rpart, rs, ag, red,
+    h_ssem, h_rsem, p_ssem, p_rsem, e_ssem, c_ssem, c_rsem, s1, r1, s2, r2, s3, r3, in_sem,
 ):
     tm = lax.axis_index("tm")
     sp = lax.axis_index("space")
@@ -61,7 +66,18 @@
     is_last = tm == tm_count - 1
     is_first = tm == 0
     blocks = cols // W
+    wf = [wf0, wf1, wf2, wf3]
+    wt = [wt0, wt1, wt2, wt3]
     skew0 = STEPS * (tm_count - 1 - tm)
+
+    loads = [
+        pltpu.make_async_copy(src, dst, in_sem.at[i])
+        for i, (src, dst) in enumerate(
+            [(states_in, states_ref), (frames_in, frames_ref), (cot_in, cot_ref), (start_in, start_ref)]
+        )
+    ]
+    for load in loads:
+        load.start()
 
     zh = jnp.zeros((MSG, W), BF16)
     z2 = jnp.zeros((2 * CH, W), BF16)
@@ -132,6 +148,8 @@
         for c in range(blocks + 1, chunks + 1):
             ref[index, c] = jnp.zeros((TILE, W), BF16)
 
+    for load in loads:
+        load.wait()
     for f in range(STEPS):
         put(zpa, f, dot(perm_a, flat(states_ref[f], CH).astype(BF16)))
         both = jnp.concatenate([flat(frames_ref[f], 3), flat(cot_ref[f], 12)], axis=0).astype(BF16)
@@ -206,19 +224,6 @@
         def _():
             h_copy(j, False).start()
 
-        @pl.when(jnp.logical_not(is_last))
-        def _():
-            qsend[j] = skewed(zpa, STEPS - 1, j, skew0 - 1)
-            p_copy(j, 0).start()
-
-            @pl.when(has_up)
-            def _():
-                p_copy(j, 1).start()
-
-            @pl.when(has_dn)
-            def _():
-                p_copy(j, 2).start()
-
         @pl.when(is_first)
         def _():
             a_val = skewed(zpa, STEPS, j, skew0 + STEPS - 1)
@@ -236,55 +241,116 @@
 
         return carry
 
-    lax.fori_loop(0, chunks, send_chunk, 0)
-
-    small = small_ref[...]
-    biasb[...] = jnp.concatenate([jnp.broadcast_to(chan_ref[:, 0:1], (CH, W))] * 16, axis=0)
-    retb[...] = jnp.concatenate([jnp.broadcast_to(chan_ref[:, 1:2], (CH, W))] * 16, axis=0)
-
-    def spread(rows, cols_n, flat_w, width, pick, at, relation):
-        r_i = iota2((rows, cols_n), 0) // CH
-        c_i = iota2((rows, cols_n), 1) // CH
-        left = onehot(lax.rem(iota2((rows, CH), 0), CH) == iota2((rows, CH), 1))
-        base = dot(left, flat_w).astype(BF16)
-        total = jnp.zeros((rows, cols_n), F32)
-        s_r = iota2((width, cols_n), 0)
-        s_c = lax.rem(iota2((width, cols_n), 1), CH)
-        for a in range(3):
-            part = dot(base, onehot(pick(a, s_r, s_c)))
-            total = jnp.where(relation(r_i, c_i) == a, part, total)
-        return total.astype(BF16)
-
-    fwd = small[:, 0:144]
-    bwd = small[:, 144:288]
-    fwd_in = small[:, 288:320]
-    head_t = small[:, 320:336]
-    bwd_in = small[:, 336:480]
-    for m in range(3):
-        b = 2 - m
-        ahead = lambda r, c: c - r
-        wa[m] = spread(256, 288, fwd, 144, lambda a, s, c: s == (3 * a + b) * CH + c, 0, ahead)
-        wb[m] = spread(256, 288, fwd_in, 32, lambda a, s, c: (s == (3 * a + b) * 3 + c) & (c < 3), 0, ahead)
-    wp[...] = spread(256, 288, head_t, 16, lambda a, s, c: (s == c - 4) & (c >= 4) & (a == 1), 0, ahead)
-    for b in range(3):
-        behind = lambda r, c: r + 2 - c
-        t_b = spread(224, 256, bwd, 144, lambda a, s, c: s == (3 * a + b) * CH + c, 0, behind)
-        rr = iota2((32, 256), 0)
-        left = onehot(rr[:, :CH] // ROWS == iota2((32, CH), 1))
-        base = dot(left, bwd_in).astype(BF16)
+    def send_previous(j, carry):
+        qsend[j] = skewed(zpa, STEPS - 1, j, skew0 - 1)
+        p_copy(j, 0).start()
+
+        @pl.when(has_up)
+        def _():
+            p_copy(j, 1).start()
+
+        @pl.when(has_dn)
+        def _():
+            p_copy(j, 2).start()
+
+        return carry
+
+    def column(ref):
+        row = ref[...].reshape(1, CH)
+        eye = iota2((CH, CH), 0) == iota2((CH, CH), 1)
+        value = jnp.sum(jnp.where(eye, row, 0.0), axis=1, keepdims=True)
+        return jnp.concatenate([jnp.broadcast_to(value, (CH, W))] * 16, axis=0)
+
+    def build_weights():
+        biasb[...] = column(bias_ref)
+        retb[...] = column(retain_ref)
+        rec = [wrec_ref[t] for t in range(9)]
+        inp = [win_ref[t] for t in range(9)]
+        chan_of = iota2((32, CH), 0) // ROWS == iota2((32, CH), 1)
+        inp_rows = [dot(onehot(chan_of[:, :3]), inp[t]).astype(BF16) for t in range(9)]
         for k in range(STEPS):
             n = 16 - 2 * k
-            first = STEPS - 1 - k
-            r_i = lax.rem(rr, ROWS)
-            c_i = iota2((32, 256), 1) // CH - first
-            total = jnp.zeros((32, 256), F32)
+            size = CH * (n + 2)
+            at = iota2((1, 6 * size), 1)
+            part = at // size
+            row_in = lax.rem(at, size) // CH
+            chan = lax.rem(at, CH)
+            picks = []
+            for m in range(3):
+                picks.append(
+                    (
+                        onehot((iota2((CH, 6 * size), 0) == chan) & (part == 2 * m)),
+                        onehot((iota2((3, 6 * size), 0) == chan) & (part == 2 * m + 1)),
+                    )
+                )
+            base = []
             for a in range(3):
-                s_r = iota2((144, 256), 0)
-                s_c = lax.rem(iota2((144, 256), 1), CH)
-                part = dot(base, onehot(s_r == (3 * a + b) * CH + s_c))
-                total = jnp.where(r_i + 2 - c_i == a, part, total)
-            wt[k, b, 0 : CH * (n - 2)] = t_b[0 : CH * (n - 2)]
-            wt[k, b, CH * (n - 2) : CH * n] = total.astype(BF16)
+                total = jnp.zeros((CH, 6 * size), F32)
+                for m in range(3):
+                    t = 3 * a + 2 - m
+                    total = total + dot(rec[t], picks[m][0]) + dot_tn(inp[t], picks[m][1])
+                base.append(total)
+            for r in range(n):
+                ahead = row_in - r
+                value = jnp.where(ahead == 0, base[0], jnp.where(ahead == 1, base[1], jnp.where(ahead == 2, base[2], 0.0)))
+                wf[k][CH * r : CH * (r + 1)] = value.astype(BF16)
+            size = CH * n
+            at = iota2((1, 3 * size), 1)
+            part = at // size
+            row_in = lax.rem(at, size) // CH
+            chan = lax.rem(at, CH)
+            picks = [onehot((iota2((CH, 3 * size), 0) == chan) & (part == b)) for b in range(3)]
+            base = []
+            base_in = []
+            for a in range(3):
+                total = jnp.zeros((CH, 3 * size), F32)
+                total_in = jnp.zeros((32, 3 * size), F32)
+                for b in range(3):
+                    t = 3 * a + b
+                    total = total + dot_tn(rec[t], picks[b])
+                    total_in = total_in + dot(inp_rows[t], picks[b])
+                base.append(total)
+                base_in.append(total_in)
+            for r in range(n - 2):
+                behind = r + 2 - row_in
+                value = jnp.where(
+                    behind == 0, base[0], jnp.where(behind == 1, base[1], jnp.where(behind == 2, base[2], 0.0))
+                )
+                wt[k][CH * r : CH * (r + 1)] = value.astype(BF16)
+            behind = lax.rem(iota2((32, 1), 0), ROWS) + 2 - (row_in - (STEPS - 1 - k))
+            value = jnp.where(
+                behind == 0, base_in[0], jnp.where(behind == 1, base_in[1], jnp.where(behind == 2, base_in[2], 0.0))
+            )
+            wt[k][CH * (n - 2) : CH * n] = value.astype(BF16)
+        pick = onehot(iota2((12, 256), 0) == lax.rem(iota2((12, 256), 1), CH) - 4)
+        base_h = dot_tn(whead_ref[...], pick)
+        for r in range(16):
+            wp[CH * r : CH * (r + 1)] = jnp.where(iota2((1, 256), 1) // CH == r, base_h, 0.0).astype(BF16)
+
+    def head_gradient():
+        total = jnp.zeros((12 * ROWS, TILE), F32)
+        for f in range(STEPS):
+            total = total + dot_nt(flat(cot_ref[f], 12).astype(BF16), flat(states_ref[f], CH).astype(BF16))
+        same = lax.rem(iota2((12 * ROWS, TILE), 0), ROWS) == lax.rem(iota2((12 * ROWS, TILE), 1), ROWS)
+        total = jnp.where(same, total, 0.0)
+        pick_l = jnp.where(iota2((CH, 12 * ROWS), 0) == iota2((CH, 12 * ROWS), 1) // ROWS, 1.0, 0.0)
+        pick_r = jnp.where(iota2((TILE, W), 0) // ROWS == iota2((TILE, W), 1), 1.0, 0.0)
+        headacc[...] = dot_exact(dot_exact(pick_l, total), pick_r)
+
+    @pl.when(is_last)
+    def _():
+        lax.fori_loop(0, chunks, send_chunk, 0)
+
+    @pl.when(jnp.logical_not(is_last))
+    def _():
+        lax.fori_loop(0, chunks, send_previous, 0)
+
+    build_weights()
+
+    @pl.when(jnp.logical_not(is_last))
+    def _():
+        head_gradient()
+        lax.fori_loop(0, chunks, send_chunk, 0)
 
     lane = iota2((1, W), 1)
 
@@ -315,19 +381,20 @@
             both = jnp.concatenate([a_now, b_now], axis=0)
             both_old = jnp.concatenate([a_old, b_old], axis=0)
             size = CH * (n + 2)
-            preact = biasb[0 : CH * n]
+            taps = []
+            low = (h - 1) * CH
             for m in range(3):
                 if m == 0:
                     x = both
                 else:
                     x = jnp.where(lane >= m, pltpu.roll(both, m, 1), pltpu.roll(both_old, m, 1))
+                taps.append(x)
                 x_a, x_b = x[:size], x[size:]
-                preact = preact + dot(wa[m, 0 : CH * n, 0:size], x_a) + dot(wb[m, 0 : CH * n, 0:size], x_b)
                 if m == 1:
-                    pushed[j, k, 0 : CH * n] = dot(wp[0 : CH * n, 0:size], x_b)
-                low = (h - 1) * CH
+                    pushed[j, k, 0 : CH * n] = dot(wp[0 : CH * n, 0 : CH * n], x_b[CH : CH + CH * n])
                 xs[j, k, m, 0 : 10 * CH] = x_a[low : low + 10 * CH]
                 xs[j, k, m, 10 * CH : 20 * CH] = x_b[low : low + 10 * CH]
+            preact = biasb[0 : CH * n] + dot(wf[k][...], jnp.concatenate(taps, axis=0))
             col = W * j + lane - (skew0 + k + 1)
             row = ROWS * sp + iota2((CH * n, 1), 0) // CH + (k - STEPS)
             inside = (col >= 0) & (col < cols) & (row >= 0) & (row < ROWS * space_count)
@@ -397,11 +464,7 @@
             inner = g[CH : size - CH]
             rg, gs = shifted(inner, gprev[k, 0 : size - 2 * CH], 1)
             gprev[k, 0 : size - 2 * CH] = rg
-            conv = (
-                dot(wt[k, 0, 0:size, 0:size], d)
-                + dot(wt[k, 1, 0:size, 0:size], d1)
-                + dot(wt[k, 2, 0:size, 0:size], d2)
-            )
+            conv = dot(wt[k][...], jnp.concatenate([d, d1, d2], axis=0))
             carried = retb[0 : size - 2 * CH] * gs + conv[0 : size - 2 * CH]
             gfs[j, k] = conv[size - 2 * CH : size]
             at = (STEPS - k) * CH
@@ -451,91 +514,95 @@
     def _():
         lax.fori_loop(0, chunks, prepare, 0)
 
-    total = jnp.zeros((12 * ROWS, TILE), F32)
-    for f in range(STEPS):
-        total = total + dot_nt(flat(cot_ref[f], 12).astype(BF16), flat(states_ref[f], CH).astype(BF16))
-    same = lax.rem(iota2((12 * ROWS, TILE), 0), ROWS) == lax.rem(iota2((12 * ROWS, TILE), 1), ROWS)
-    total = jnp.where(same, total, 0.0)
-    pick_l = jnp.where(iota2((CH, 12 * ROWS), 0) == iota2((CH, 12 * ROWS), 1) // ROWS, 1.0, 0.0)
-    pick_r = jnp.where(iota2((TILE, W), 0) // ROWS == iota2((TILE, W), 1), 1.0, 0.0)
-    headacc[...] = dot_exact(dot_exact(pick_l, total), pick_r)
-
     lax.fori_loop(0, chunks, step, 0)
 
     @pl.when(is_last)
     def _():
         lax.fori_loop(0, chunks, post, 0)
-
-    rpart[0:48, 0:64] = gram[0:48]
-    rpart[0:48, 64:128] = gram[48:96]
-    rpart[48:64] = headacc[...]
-    piece = 64 // tm_count
-
-    def cut(t):
-        return pl.ds(pl.multiple_of(t * piece, 8), piece)
+        head_gradient()
+
+    rpart[0:16, 0:64] = gram[0:16]
+    rpart[0:16, 64:128] = gram[16:32]
+    rpart[16:32, 0:64] = gram[32:48]
+    rpart[16:32, 64:80] = headacc[:, 0:CH]
+    rpart[16:24, 80:128] = gram[80:88, 0:48]
+    rpart[24:32, 80:128] = jnp.zeros((8, 48), F32)
+    rpart[32:40, 0:64] = gram[48:56]
+    rpart[32:40, 64:128] = gram[64:72]
 
     def first_copy(p):
-        t = lax.rem(tm + p, tm_count)
         return pltpu.make_async_remote_copy(
-            src_ref=rpart.at[cut(t)], dst_ref=rs.at[p], send_sem=s1.at[p], recv_sem=r1.at[p],
-            device_id=(t, sp), device_id_type=MESH,
+            src_ref=rpart, dst_ref=rs.at[p], send_sem=s1.at[0], recv_sem=r1.at[p],
+            device_id=(0, sp), device_id_type=MESH,
         )
 
-    for p in range(1, tm_count):
-        first_copy(p).start()
+    @pl.when(jnp.logical_not(is_first))
+    def _():
+        first_copy(tm).start()
 
     out_shift = skew0 + STEPS + 1
-    for c in range(blocks):
-        def unskew(now, after, shift):
-            return jnp.where(lane < W - shift, pltpu.roll(now, W - shift, 1), pltpu.roll(after, W - shift, 1))
-
-        value = unskew(bnd[c], bnd[c + 1], out_shift)
-        for r in range(ROWS):
-            bound_ref[r, :, W * c : W * (c + 1)] = value[CH * r : CH * (r + 1)]
-        for k in range(STEPS):
-            value = unskew(gfs[c, k, 0:24], gfs[c + 1, k, 0:24], skew0 + k + 2)
-            gf_ref[STEPS - 1 - k, :, :, W * c : W * (c + 1)] = value.reshape(3, ROWS, W).astype(BF16)
-
-    part = rpart[cut(tm)]
-    for p in range(1, tm_count):
-        first_copy(p).wait_recv()
-        part = part + rs[p]
-    ag[sp] = part
+
+    def put_outputs():
+        for c in range(blocks):
+            def unskew(now, after, shift):
+                return jnp.where(lane < W - shift, pltpu.roll(now, W - shift, 1), pltpu.roll(after, W - shift, 1))
+
+            value = unskew(bnd[c], bnd[c + 1], out_shift)
+            for r in range(ROWS):
+                bound_ref[0, :, r, W * c : W * (c + 1)] = value[CH * r : CH * (r + 1)]
+            for k in range(STEPS):
+                value = unskew(gfs[c, k, 0:24], gfs[c + 1, k, 0:24], skew0 + k + 2)
+                gf_ref[STEPS - 1 - k, :, :, W * c : W * (c + 1)] = value.reshape(3, ROWS, W).astype(BF16)
 
     def second_copy(q):
         s = lax.rem(sp + q, space_count)
         return pltpu.make_async_remote_copy(
             src_ref=ag.at[sp], dst_ref=ag.at[sp], send_sem=s2.at[q], recv_sem=r2.at[q],
-            device_id=(tm, s), device_id_type=MESH,
+            device_id=(0, s), device_id_type=MESH,
         )
 
-    for q in range(1, space_count):
-        second_copy(q).start()
-    for q in range(1, space_count):
-        second_copy(q).wait_recv()
-    part = ag[0]
-    for q in range(1, space_count):
-        part = part + ag[q]
-    red[cut(tm)] = part
-
-    def third_copy(p):
-        t = lax.rem(tm + p, tm_count)
+    def third_copy(t):
         return pltpu.make_async_remote_copy(
-            src_ref=red.at[cut(tm)], dst_ref=red.at[cut(tm)], send_sem=s3.at[p], recv_sem=r3.at[p],
+            src_ref=red, dst_ref=red, send_sem=s3.at[t], recv_sem=r3.at[0],
             device_id=(t, sp), device_id_type=MESH,
         )
 
-    for p in range(1, tm_count):
-        third_copy(p).start()
-    for p in range(1, tm_count):
-        third_copy(p).wait_recv()
+    @pl.when(is_first)
+    def _():
+        part = rpart[...]
+        for t in range(1, tm_count):
+            first_copy(t).wait_recv()
+            part = part + rs[t]
+        ag[sp] = part
+        for q in range(1, space_count):
+            second_copy(q).start()
+        put_outputs()
+        for q in range(1, space_count):
+            second_copy(q).wait_recv()
+        part = ag[0]
+        for q in range(1, space_count):
+            part = part + ag[q]
+        red[...] = part
+        for t in range(1, tm_count):
+            third_copy(t).start()
+
+    @pl.when(jnp.logical_not(is_first))
+    def _():
+        put_outputs()
+        third_copy(1).wait_recv()
+
     sums_ref[...] = red[...]
 
-    for p in range(1, tm_count):
-        first_copy(p).wait_send()
-        third_copy(p).wait_send()
-    for q in range(1, space_count):
-        second_copy(q).wait_send()
+    @pl.when(is_first)
+    def _():
+        for q in range(1, space_count):
+            second_copy(q).wait_send()
+        for t in range(1, tm_count):
+            third_copy(t).wait_send()
+
+    @pl.when(jnp.logical_not(is_first))
+    def _():
+        first_copy(tm).wait_send()
 
     def drain(j, carry):
         @pl.when(has_up)
@@ -583,27 +650,40 @@
         return carry
 
     lax.fori_loop(0, chunks, drain, 0)
+
+
+def finish(sums_ref, gf_in, bound_in, rec_ref, in_ref, bias_ref, keep_ref, head_ref, gf_ref, bound_ref, sem):
+    moves = [pltpu.make_async_copy(gf_in, gf_ref, sem.at[0]), pltpu.make_async_copy(bound_in, bound_ref, sem.at[1])]
+    for move in moves:
+        move.start()
+    sums = sums_ref[...]
+    turned = jnp.concatenate([sums, jnp.zeros((W - 40, W), F32)], axis=0).T
+    for m in range(3):
+        b = 2 - m
+        lane_rec, row_rec = [(0, 0), (64, 0), (0, 16)][m]
+        lane_in, row_in = [(0, 32), (64, 32), (80, 16)][m]
+        for a in range(3):
+            rec_ref[3 * a + b] = turned[lane_rec + CH * a : lane_rec + CH * (a + 1), row_rec : row_rec + CH]
+            in_ref[3 * a + b] = sums[row_in : row_in + 3, lane_in + CH * a : lane_in + CH * (a + 1)]
+    bias_ref[...] = sums[35:36, 80:96].reshape(CH)
+    eye = iota2((CH, CH), 0) == iota2((CH, CH), 1)
+    keep_ref[...] = jnp.sum(jnp.where(eye, sums[0:16, 112:128], 0.0), axis=0, keepdims=True).reshape(CH)
+    head_ref[...] = sums[16:28, 64:80]
+    for move in moves:
+        move.wait()
 
 
 def on_device(tm_count, space_count, frames, states, start_state, cotangent, w_rec, w_in, bias_vec, retain, w_head):
     cols = states.shape[3]
     chunks = -(-(cols + STEPS * tm_count + 1) // W)
-    pad = lambda value, rows, width: jnp.pad(value, ((0, rows - value.shape[0]), (0, width - value.shape[1])))
-    small = jnp.concatenate(
-        [
-            w_rec.reshape(16, 144),
-            w_rec.transpose(2, 1, 0).reshape(16, 144),
-            pad(w_in.reshape(16, 27), 16, 32),
-            pad(w_head.T, 16, 16),
-            pad(w_in.transpose(2, 1, 0).reshape(3, 144), 16, 144),
-        ],
-        axis=1,
-    )
-    small = pad(small, 16, 512)
-    chan = jnp.stack([bias_vec, retain], axis=1)
     vmem = pl.BlockSpec(memory_space=pltpu.VMEM)
+    anywhere = pl.BlockSpec(memory_space=pl.ANY)
     dma = pltpu.SemaphoreType.DMA
     scratch = [
+        pltpu.VMEM(frames.shape, BF16),
+        pltpu.VMEM(states.shape, BF16),
+        pltpu.VMEM(start_state.shape, BF16),
+        pltpu.VMEM(cotangent.shape, BF16),
         pltpu.VMEM((STEPS + 1, chunks + 1, TILE, W), BF16),
         pltpu.VMEM((STEPS, chunks + 1, TILE, W), BF16),
         pltpu.VMEM((chunks + 1, STEPS, TILE, W), BF16),
@@ -628,10 +708,9 @@
         pltpu.VMEM((chunks, STEPS * CH, W), BF16),
         pltpu.VMEM((chunks, STEPS * CH, W), BF16),
         pltpu.VMEM((chunks, TILE, W), BF16),
-        pltpu.VMEM((3, 256, 288), BF16),
-        pltpu.VMEM((3, 256, 288), BF16),
-        pltpu.VMEM((256, 288), BF16),
-        pltpu.VMEM((STEPS, 3, 256, 256), BF16),
+        *[pltpu.VMEM((CH * n, 6 * CH * (n + 2)), BF16) for n in (16, 14, 12, 10)],
+        pltpu.VMEM((256, 256), BF16),
+        *[pltpu.VMEM((CH * n, 3 * CH * n), BF16) for n in (16, 14, 12, 10)],
         pltpu.VMEM((STEPS, 256, W), BF16),
         pltpu.VMEM((STEPS, 256, W), BF16),
         pltpu.VMEM((STEPS, 256, W), F32),
@@ -639,44 +718,50 @@
         pltpu.VMEM((256, W), F32),
         pltpu.VMEM((96, 64), F32),
         pltpu.VMEM((CH, W), F32),
-        pltpu.VMEM((64, W), F32),
-        pltpu.VMEM((tm_count, 64 // tm_count, W), F32),
-        pltpu.VMEM((space_count, 64 // tm_count, W), F32),
-        pltpu.VMEM((64, W), F32),
+        pltpu.VMEM((40, W), F32),
+        pltpu.VMEM((tm_count, 40, W), F32),
+        pltpu.VMEM((space_count, 40, W), F32),
+        pltpu.VMEM((40, W), F32),
         dma((2, chunks)), dma((2, chunks)),
         dma((3, chunks)), dma((3, chunks)), dma((3, chunks)),
         dma((3, chunks)), dma((3, chunks)),
         dma((tm_count,)), dma((tm_count,)),
         dma((space_count,)), dma((space_count,)),
-        dma((tm_count,)), dma((tm_count,)),
+        dma((tm_count,)), dma((tm_count,)), dma((4,)),
     ]
     grad_frames, bound, sums = pl.pallas_call(
         functools.partial(kernel, tm_count, space_count, cols, chunks),
         out_shape=[
             jax.ShapeDtypeStruct((STEPS, 3, ROWS, cols), BF16),
-            jax.ShapeDtypeStruct((ROWS, CH, cols), F32),
-            jax.ShapeDtypeStruct((64, W), F32),
+            jax.ShapeDtypeStruct((1, CH, ROWS, cols), F32),
+            jax.ShapeDtypeStruct((40, W), F32),
         ],
-        in_specs=[vmem] * 6,
+        in_specs=[anywhere] * 4 + [vmem] * 5,
         out_specs=[vmem] * 3,
         scratch_shapes=scratch,
         compiler_params=pltpu.CompilerParams(
             collective_id=0, has_side_effects=True, vmem_limit_bytes=56 * 1024 * 1024
         ),
-    )(frames, states, start_state, cotangent, small, chan)
-    def taps(block, width):
-        parts = block[:, :, 0:48].reshape(3, CH, 3, CH)[::-1, :width]
-        return parts.transpose(3, 2, 0, 1).reshape(CH, 9, width)
-
-    rec = sums[0:48, 0:64].reshape(3, CH, 64)
-    other = sums[0:48, 64:128].reshape(3, CH, 64)
-    grad_rec = taps(rec, CH)
-    grad_in = taps(other, 3)
-    grad_bias = other[1, 3, 16:32]
-    eye = jnp.eye(CH, dtype=bool)
-    grad_retain = jnp.sum(jnp.where(eye, rec[1, :, 48:64], 0.0), axis=0)
-    grad_head = sums[48:60, 0:16]
-    return (grad_rec, grad_in, grad_bias, grad_retain, grad_head, grad_frames, bound.transpose(1, 0, 2)[None])
+    )(
+        frames, states, start_state, cotangent, w_rec.transpose(1, 0, 2), w_in.transpose(1, 2, 0), bias_vec, retain, w_head
+    )
+    out_shape = [
+        jax.ShapeDtypeStruct((9, CH, CH), F32),
+        jax.ShapeDtypeStruct((9, 3, CH), F32),
+        jax.ShapeDtypeStruct((CH,), F32),
+        jax.ShapeDtypeStruct((CH,), F32),
+        jax.ShapeDtypeStruct((12, CH), F32),
+        jax.ShapeDtypeStruct(grad_frames.shape, BF16),
+        jax.ShapeDtypeStruct(bound.shape, F32),
+    ]
+    rec, inp, *rest = pl.pallas_call(
+        finish,
+        out_shape=out_shape,
+        in_specs=[vmem, vmem, vmem],
+        out_specs=[vmem] * 5 + [anywhere] * 2,
+        scratch_shapes=[dma((2,))],
+    )(sums, grad_frames, bound)
+    return (rec.transpose(1, 0, 2), inp.transpose(2, 0, 1), *rest)
 
 
 def solution(mesh):

time: 104 us -> 89.2 us (0.86)
  local copies, waits for them, and re-layouts: 8.87 us -> 0 us
  Pallas kernels: 92.8 us -> 88.1 us
  other arithmetic: 1.29 us -> 0 us
    pallas_call x1, Pallas kernels: 92.8 us -> 85.5 us  [on_device(): pl.pallas_call(functools.partial(kernel, tm_count, space_count, cols, chu...]
    unnamed x12 -> x0, local copies, waits for them, and re-layouts: 4.3 us -> none
    pallas_call x0 -> x1, Pallas kernels: none -> 2.55 us  [on_device(): pl.pallas_call(finish, out_shape=out_shape, in_specs=[vmem, vmem, vmem],...]
    transpose x5 -> x0, local copies, waits for them, and re-layouts: 1.37 us -> none  [the longest x4 1.36 us: taps(): return parts.transpose(3, 2, 0, 1).reshape(CH, 9, width)]
where the time goes in v2:
time: 89.2 us; the launch traced here: 88.7 us
  Pallas kernels  88.1 us (99%)
    pallas_call x1, Pallas kernels, on_device(): pl.pallas_call(functools.partial(kernel, tm_count, space_count, cols, chu...  85.5 us
    pallas_call x1, Pallas kernels, on_device(): pl.pallas_call(finish, out_shape=out_shape, in_specs=[vmem, vmem, vmem],...  2.55 us

profile of v2, /device:TPU:1, one launch (start us, length us, event | category | flops | bytes accessed | tf_op | source)
XLA Modules:
  0.0 88.7 jit_solution(1712460567388407206)
XLA Ops:
  0.6 85.5 %shard_map.144 = (bf16[4,3,8,768]{3,2,1,0:T(8,128)(2,1)}, f32[1,16,8,768]{3,2,1,0:T(8,128)}, f32[40,128]{1,0:T(8,128)}) custom-call(bf16[4,3,8,768]{3,2,1,0:T(8,128)(2,1)} %frames_in.1, bf16[4,16,8,768]{3,2,1,0:T(8,128)(2,1)} %states_in.1, bf16[16,8,768]{2,1,0:T(8,128)(2,1)} %start_in.1, bf16[4,12,8,768]{3,2,1,0:T(8,128)(2,1)} %cot_in.1, ...), custom_call_target="tpu_custom_call" | custom-call | tf_op jit(solution)/shard_map/pallas_call | solution.py:732
  86.2 2.6 %shard_map.145 = (f32[9,16,16]{2,1,0:T(8,128)}, f32[9,3,16]{2,1,0:T(4,128)}, f32[16]{0:T(128)}, f32[16]{0:T(128)}, f32[12,16]{1,0:T(8,128)}, /*index=5*/bf16[4,3,8,768]{3,2,1,0:T(8,128)(2,1)}, f32[1,16,8,768]{3,2,1,0:T(8,128)}) custom-call(f32[40,128]{1,0:T(8,128)} %get-tuple-element.17.sums_ref, bf16[4,3,8,768]{3,2,1,0:T(8,128)(2,1)} %get-tuple-element.18.gf_in, ...), custom_call_target="tpu_custom_call" | custom-call | tf_op jit(solution)/shard_map/pallas_call | solution.py:757

commit v3 on v2

--- a/solution.py
+++ b/solution.py
@@ -54,8 +54,8 @@
     frames_in, states_in, start_in, cot_in, wrec_ref, win_ref, bias_ref, retain_ref, whead_ref,
     gf_ref, bound_ref, sums_ref,
     frames_ref, states_ref, start_ref, cot_ref,
-    zpa, zpb, za, zb, qsend, stage_up, stage_dn, h_up, h_dn, p_up, p_dn, p_stage_up, p_stage_dn,
-    slopes, pushed, xs, dkeep, gkeep, gfs, bnd, c_own, c_up, c_dn, c_send,
+    zpa, zpb, zpq, stage_up, stage_dn, h_up, h_dn, p_up, p_dn, oldx,
+    slopes, pushed, xs, dkeep, gkeep, gfs, bnd, c_own, c_up, c_dn, c_send, l_own, l_up, l_dn, l_send,
     wf0, wf1, wf2, wf3, wp, wt0, wt1, wt2, wt3, d1prev, d2prev, gprev, biasb, retb, gram, headacc, rpart, rs, ag, red,
     h_ssem, h_rsem, p_ssem, p_rsem, e_ssem, c_ssem, c_rsem, s1, r1, s2, r2, s3, r3, in_sem,
 ):
@@ -65,6 +65,7 @@
     has_dn = sp < space_count - 1
     is_last = tm == tm_count - 1
     is_first = tm == 0
+    is_early = tm >= tm_count - 1
     blocks = cols // W
     wf = [wf0, wf1, wf2, wf3]
     wt = [wt0, wt1, wt2, wt3]
@@ -81,13 +82,19 @@
 
     zh = jnp.zeros((MSG, W), BF16)
     z2 = jnp.zeros((2 * CH, W), BF16)
-    h_up[0] = zh
-    h_dn[0] = zh
-    p_up[0] = z2
-    p_dn[0] = z2
+    zt = jnp.zeros((TILE, W), BF16)
+    for slot in [0] + list(range(blocks + 1, chunks + 1)):
+        h_up[slot] = zh
+        h_dn[slot] = zh
+        p_up[slot] = z2
+        p_dn[slot] = z2
+        zpq[slot] = zt
+        for f in range(STEPS):
+            zpa[f, slot] = zt
+            zpb[f, slot] = zt
     for k in range(STEPS):
-        za[0, k] = jnp.zeros((TILE, W), BF16)
-        zb[0, k] = jnp.zeros((TILE, W), BF16)
+        for m in range(3):
+            oldx[k, m] = jnp.zeros((36 * CH, W), BF16)
         gprev[k] = jnp.zeros((16 * CH, W), F32)
         d1prev[k] = jnp.zeros((16 * CH, W), BF16)
         d2prev[k] = jnp.zeros((16 * CH, W), BF16)
@@ -95,21 +102,28 @@
 
     @pl.when(jnp.logical_not(has_up))
     def _():
-        for j in range(chunks):
+        for j in range(blocks):
             h_up[j + 1] = zh
             p_up[j + 1] = z2
+        l_up[...] = z2
+        for j in range(blocks):
             c_up[j] = jnp.zeros((STEPS * CH, W), BF16)
 
     @pl.when(jnp.logical_not(has_dn))
     def _():
-        for j in range(chunks):
+        for j in range(blocks):
             h_dn[j + 1] = zh
             p_dn[j + 1] = z2
+        l_dn[...] = z2
+        for j in range(blocks):
             c_dn[j] = jnp.zeros((STEPS * CH, W), BF16)
 
     @pl.when(is_last)
     def _():
-        for j in range(chunks):
+        l_own[...] = z2
+        l_up[...] = z2
+        l_dn[...] = z2
+        for j in range(blocks):
             c_own[j] = jnp.zeros((TILE, W), BF16)
             c_up[j] = jnp.zeros((STEPS * CH, W), BF16)
             c_dn[j] = jnp.zeros((STEPS * CH, W), BF16)
@@ -140,24 +154,21 @@
     def flat(value, channels):
         return value.astype(F32).reshape(channels * ROWS, cols)
 
-    def put(ref, index, value):
+    def put(ref, value):
         value = value.astype(BF16)
-        ref[index, 0] = jnp.zeros((TILE, W), BF16)
         for c in range(blocks):
-            ref[index, c + 1] = value[:, W * c : W * (c + 1)]
-        for c in range(blocks + 1, chunks + 1):
-            ref[index, c] = jnp.zeros((TILE, W), BF16)
+            ref[c + 1] = value[:, W * c : W * (c + 1)]
 
     for load in loads:
         load.wait()
     for f in range(STEPS):
-        put(zpa, f, dot(perm_a, flat(states_ref[f], CH).astype(BF16)))
+        put(zpa.at[f], dot(perm_a, flat(states_ref[f], CH).astype(BF16)))
         both = jnp.concatenate([flat(frames_ref[f], 3), flat(cot_ref[f], 12)], axis=0).astype(BF16)
-        put(zpb, f, dot(perm_b, both) + ones_b)
+        put(zpb.at[f], dot(perm_b, both) + ones_b)
 
     @pl.when(is_first)
     def _():
-        put(zpa, STEPS, dot(perm_a, flat(start_ref[...], CH).astype(BF16)))
+        put(zpq, dot(perm_a, flat(start_ref[...], CH).astype(BF16)))
 
     pl.semaphore_wait(barrier, tm_count - 1 + space_count - 1 + 4)
 
@@ -170,20 +181,20 @@
         )
 
     def p_copy(j, way):
-        src = [qsend.at[j], qsend.at[j, pl.ds(0, 2 * CH)], qsend.at[j, pl.ds(6 * CH, 2 * CH)]][way]
-        dst = [za.at[j + 1, STEPS - 1], p_dn.at[j + 1], p_up.at[j + 1]][way]
+        rows = [pl.ds(0, TILE), pl.ds(0, 2 * CH), pl.ds(6 * CH, 2 * CH)][way]
+        dst = [zpq.at[j + 1], p_dn.at[j + 1], p_up.at[j + 1]][way]
         target = (tm + 1, [sp, sp - 1, sp + 1][way])
         return pltpu.make_async_remote_copy(
-            src_ref=src, dst_ref=dst, send_sem=p_ssem.at[way, j], recv_sem=p_rsem.at[way, j],
+            src_ref=zpa.at[STEPS - 1, j + 1, rows], dst_ref=dst, send_sem=p_ssem.at[way, j], recv_sem=p_rsem.at[way, j],
             device_id=target, device_id_type=MESH,
         )
 
     def s_copy(j, way):
-        src = [None, p_stage_up.at[j], p_stage_dn.at[j]][way]
+        rows = [None, pl.ds(0, 2 * CH), pl.ds(6 * CH, 2 * CH)][way]
         dst = [None, p_dn.at[j + 1], p_up.at[j + 1]][way]
         target = (tm, [sp, sp - 1, sp + 1][way])
         return pltpu.make_async_remote_copy(
-            src_ref=src, dst_ref=dst, send_sem=e_ssem.at[way, j], recv_sem=p_rsem.at[way, j],
+            src_ref=zpq.at[j + 1, rows], dst_ref=dst, send_sem=e_ssem.at[way, j], recv_sem=p_rsem.at[way, j],
             device_id=target, device_id_type=MESH,
         )
 
@@ -196,23 +207,26 @@
             device_id=target, device_id_type=MESH,
         )
 
-    def skewer(shift):
-        return onehot(iota2((2 * W, W), 0) == iota2((2 * W, W), 1) + (W - shift))
-
-    def skewed(ref, index, j, shift):
-        wide = jnp.concatenate([ref[index, j], ref[index, j + 1]], axis=1)
-        return dot(wide, skewer(shift)).astype(BF16)
-
     def send_chunk(j, carry):
+        @pl.when(jnp.logical_not(is_last))
+        def _():
+            @pl.when(has_up)
+            def _():
+                p_copy(j, 1).start()
+
+            @pl.when(has_dn)
+            def _():
+                p_copy(j, 2).start()
+
+            p_copy(j, 0).start()
+
         for k in range(STEPS):
             h = HALO[k]
-            b_val = skewed(zpb, STEPS - 1 - k, j, skew0 + k)
-            zb[j + 1, k] = b_val
+            b_val = zpb[STEPS - 1 - k, j + 1]
             stage_up[j, B_AT[k] * CH : (B_AT[k] + h) * CH] = b_val[: h * CH]
             stage_dn[j, B_AT[k] * CH : (B_AT[k] + h) * CH] = b_val[TILE - h * CH :]
             if k < STEPS - 1:
-                a_val = skewed(zpa, STEPS - 2 - k, j, skew0 + k)
-                za[j + 1, k] = a_val
+                a_val = zpa[STEPS - 2 - k, j + 1]
                 stage_up[j, A_AT[k] * CH : (A_AT[k] + h) * CH] = a_val[: h * CH]
                 stage_dn[j, A_AT[k] * CH : (A_AT[k] + h) * CH] = a_val[TILE - h * CH :]
 
@@ -226,11 +240,6 @@
 
         @pl.when(is_first)
         def _():
-            a_val = skewed(zpa, STEPS, j, skew0 + STEPS - 1)
-            za[j + 1, STEPS - 1] = a_val
-            p_stage_up[j] = a_val[: 2 * CH]
-            p_stage_dn[j] = a_val[6 * CH :]
-
             @pl.when(has_up)
             def _():
                 s_copy(j, 1).start()
@@ -241,19 +250,13 @@
 
         return carry
 
-    def send_previous(j, carry):
-        qsend[j] = skewed(zpa, STEPS - 1, j, skew0 - 1)
-        p_copy(j, 0).start()
-
-        @pl.when(has_up)
-        def _():
-            p_copy(j, 1).start()
-
-        @pl.when(has_dn)
-        def _():
-            p_copy(j, 2).start()
-
-        return carry
+    def l_copy(way):
+        dst = [l_own, l_dn, l_up][way]
+        target = (tm - 1, [sp, sp - 1, sp + 1][way])
+        return pltpu.make_async_remote_copy(
+            src_ref=l_send, dst_ref=dst, send_sem=c_ssem.at[way, blocks], recv_sem=c_rsem.at[way, blocks],
+            device_id=target, device_id_type=MESH,
+        )
 
     def column(ref):
         row = ref[...].reshape(1, CH)
@@ -337,20 +340,8 @@
         pick_r = jnp.where(iota2((TILE, W), 0) // ROWS == iota2((TILE, W), 1), 1.0, 0.0)
         headacc[...] = dot_exact(dot_exact(pick_l, total), pick_r)
 
-    @pl.when(is_last)
-    def _():
-        lax.fori_loop(0, chunks, send_chunk, 0)
-
-    @pl.when(jnp.logical_not(is_last))
-    def _():
-        lax.fori_loop(0, chunks, send_previous, 0)
-
+    lax.fori_loop(0, blocks, send_chunk, 0)
     build_weights()
-
-    @pl.when(jnp.logical_not(is_last))
-    def _():
-        head_gradient()
-        lax.fori_loop(0, chunks, send_chunk, 0)
 
     lane = iota2((1, W), 1)
 
@@ -371,23 +362,18 @@
                     up_a, dn_a = p_up[slot], p_dn[slot]
                 up_b = h_up[slot, B_AT[k] * CH : (B_AT[k] + h) * CH]
                 dn_b = h_dn[slot, B_AT[k] * CH : (B_AT[k] + h) * CH]
-                return (
-                    jnp.concatenate([up_a, za[slot, k], dn_a], axis=0),
-                    jnp.concatenate([up_b, zb[slot, k], dn_b], axis=0),
-                )
-
-            a_now, b_now = whole(j + 1)
-            a_old, b_old = whole(j)
-            both = jnp.concatenate([a_now, b_now], axis=0)
-            both_old = jnp.concatenate([a_old, b_old], axis=0)
+                own_a = zpa[STEPS - 2 - k, slot] if k < STEPS - 1 else zpq[slot]
+                return jnp.concatenate([up_a, own_a, dn_a, up_b, zpb[STEPS - 1 - k, slot], dn_b], axis=0)
+
+            raw = whole(j + 1)
             size = CH * (n + 2)
             taps = []
             low = (h - 1) * CH
             for m in range(3):
-                if m == 0:
-                    x = both
-                else:
-                    x = jnp.where(lane >= m, pltpu.roll(both, m, 1), pltpu.roll(both_old, m, 1))
+                turn = skew0 + k + m
+                moved = pltpu.roll(raw, turn, 1)
+                x = jnp.where(lane >= turn, moved, oldx[k, m, 0 : 2 * size])
+                oldx[k, m, 0 : 2 * size] = moved
                 taps.append(x)
                 x_a, x_b = x[:size], x[size:]
                 if m == 1:
@@ -423,7 +409,10 @@
             p_copy(j, 2).wait_recv()
 
     def prepare(j, carry):
-        await_inputs(j)
+        @pl.when(j < blocks)
+        def _():
+            await_inputs(j)
+
         get_slopes(j)
         return carry
 
@@ -450,8 +439,19 @@
             gram[...] += dot_nt(left, right)
         return carry
 
-    def chain(j):
-        carried = jnp.concatenate([c_up[j], c_own[j], c_dn[j]], axis=0).astype(F32)
+    group = 2 * CH
+    spread_w = W // 4
+
+    def unpack(ref, which):
+        value = ref[...]
+        return [value if q == 0 else pltpu.roll(value, W - spread_w * q, 1) for q in which]
+
+    def chain(j, last):
+        if last:
+            parts = unpack(l_up, (2, 3)) + unpack(l_own, (0, 1, 2, 3)) + unpack(l_dn, (0, 1))
+        else:
+            parts = [c_up[j], c_own[j], c_dn[j]]
+        carried = jnp.concatenate(parts, axis=0).astype(F32)
         for k in range(STEPS):
             n = 16 - 2 * k
             size = CH * n
@@ -470,53 +470,66 @@
             at = (STEPS - k) * CH
             dkeep[j, k] = d[at : at + TILE]
             gkeep[j, k] = g[at : at + TILE].astype(BF16)
+        out = carried.astype(BF16)
+        if last:
+            packed = out[0:group]
+            for q in range(1, 4):
+                packed = jnp.where(
+                    lane >= spread_w * q, pltpu.roll(out[group * q : group * (q + 1)], spread_w * q, 1), packed
+                )
+            l_send[...] = packed
+        else:
+            c_send[j] = out
         bnd[j] = carried
-        c_send[j] = carried.astype(BF16)
-
-    def step(j, carry):
-        @pl.when(is_last)
+
+    def step(j, carry, last=False):
+        hop = l_copy if last else functools.partial(c_copy, j)
+
+        @pl.when(is_early)
         def _():
             prepare(j, 0)
 
         @pl.when(jnp.logical_not(is_last))
         def _():
-            c_copy(j, 0).wait_recv()
+            hop(0).wait_recv()
 
             @pl.when(has_dn)
             def _():
-                c_copy(j, 1).wait_recv()
+                hop(1).wait_recv()
 
             @pl.when(has_up)
             def _():
-                c_copy(j, 2).wait_recv()
-
-        chain(j)
+                hop(2).wait_recv()
+
+        chain(j, last)
 
         @pl.when(jnp.logical_not(is_first))
         def _():
-            c_copy(j, 0).start()
-
             @pl.when(has_up)
             def _():
-                c_copy(j, 1).start()
+                hop(1).start()
 
             @pl.when(has_dn)
             def _():
-                c_copy(j, 2).start()
-
-        @pl.when(jnp.logical_not(is_last))
+                hop(2).start()
+
+            hop(0).start()
+
+        @pl.when(jnp.logical_not(is_early))
         def _():
             post(j, 0)
 
         return carry
 
-    @pl.when(jnp.logical_not(is_last))
-    def _():
+    @pl.when(jnp.logical_not(is_early))
+    def _():
+        head_gradient()
         lax.fori_loop(0, chunks, prepare, 0)
 
-    lax.fori_loop(0, chunks, step, 0)
-
-    @pl.when(is_last)
+    lax.fori_loop(0, blocks, step, 0)
+    step(blocks, 0, True)
+
+    @pl.when(is_early)
     def _():
         lax.fori_loop(0, chunks, post, 0)
         head_gradient()
@@ -635,21 +648,29 @@
             def _():
                 s_copy(j, 2).wait_send()
 
-        @pl.when(jnp.logical_not(is_first))
-        def _():
-            c_copy(j, 0).wait_send()
-
-            @pl.when(has_up)
-            def _():
-                c_copy(j, 1).wait_send()
-
-            @pl.when(has_dn)
-            def _():
-                c_copy(j, 2).wait_send()
-
         return carry
 
-    lax.fori_loop(0, chunks, drain, 0)
+    lax.fori_loop(0, blocks, drain, 0)
+
+    @pl.when(jnp.logical_not(is_first))
+    def _():
+        def drain_carried(way):
+            def body(j, carry):
+                c_copy(j, way).wait_send()
+                return carry
+
+            lax.fori_loop(0, blocks, body, 0)
+            l_copy(way).wait_send()
+
+        drain_carried(0)
+
+        @pl.when(has_up)
+        def _():
+            drain_carried(1)
+
+        @pl.when(has_dn)
+        def _():
+            drain_carried(2)
 
 
 def finish(sums_ref, gf_in, bound_in, rec_ref, in_ref, bias_ref, keep_ref, head_ref, gf_ref, bound_ref, sem):
@@ -676,6 +697,7 @@
 def on_device(tm_count, space_count, frames, states, start_state, cotangent, w_rec, w_in, bias_vec, retain, w_head):
     cols = states.shape[3]
     chunks = -(-(cols + STEPS * tm_count + 1) // W)
+    blocks = cols // W
     vmem = pl.BlockSpec(memory_space=pltpu.VMEM)
     anywhere = pl.BlockSpec(memory_space=pl.ANY)
     dma = pltpu.SemaphoreType.DMA
@@ -684,19 +706,16 @@
         pltpu.VMEM(states.shape, BF16),
         pltpu.VMEM(start_state.shape, BF16),
         pltpu.VMEM(cotangent.shape, BF16),
-        pltpu.VMEM((STEPS + 1, chunks + 1, TILE, W), BF16),
         pltpu.VMEM((STEPS, chunks + 1, TILE, W), BF16),
-        pltpu.VMEM((chunks + 1, STEPS, TILE, W), BF16),
-        pltpu.VMEM((chunks + 1, STEPS, TILE, W), BF16),
-        pltpu.VMEM((chunks, TILE, W), BF16),
-        pltpu.VMEM((chunks, MSG, W), BF16),
-        pltpu.VMEM((chunks, MSG, W), BF16),
+        pltpu.VMEM((STEPS, chunks + 1, TILE, W), BF16),
+        pltpu.VMEM((chunks + 1, TILE, W), BF16),
+        pltpu.VMEM((blocks, MSG, W), BF16),
+        pltpu.VMEM((blocks, MSG, W), BF16),
         pltpu.VMEM((chunks + 1, MSG, W), BF16),
         pltpu.VMEM((chunks + 1, MSG, W), BF16),
         pltpu.VMEM((chunks + 1, 2 * CH, W), BF16),
         pltpu.VMEM((chunks + 1, 2 * CH, W), BF16),
-        pltpu.VMEM((chunks, 2 * CH, W), BF16),
-        pltpu.VMEM((chunks, 2 * CH, W), BF16),
+        pltpu.VMEM((STEPS, 3, 36 * CH, W), BF16),
         pltpu.VMEM((chunks, STEPS, 256, W), F32),
         pltpu.VMEM((chunks, STEPS, 256, W), F32),
         pltpu.VMEM((chunks, STEPS, 3, 20 * CH, W), BF16),
@@ -704,10 +723,11 @@
         pltpu.VMEM((chunks, STEPS, TILE, W), BF16),
         pltpu.VMEM((chunks, STEPS, 32, W), F32),
         pltpu.VMEM((chunks, TILE, W), F32),
-        pltpu.VMEM((chunks, TILE, W), BF16),
-        pltpu.VMEM((chunks, STEPS * CH, W), BF16),
-        pltpu.VMEM((chunks, STEPS * CH, W), BF16),
-        pltpu.VMEM((chunks, TILE, W), BF16),
+        pltpu.VMEM((blocks, TILE, W), BF16),
+        pltpu.VMEM((blocks, STEPS * CH, W), BF16),
+        pltpu.VMEM((blocks, STEPS * CH, W), BF16),
+        pltpu.VMEM((blocks, TILE, W), BF16),
+        *[pltpu.VMEM((2 * CH, W), BF16)] * 4,
         *[pltpu.VMEM((CH * n, 6 * CH * (n + 2)), BF16) for n in (16, 14, 12, 10)],
         pltpu.VMEM((256, 256), BF16),
         *[pltpu.VMEM((CH * n, 3 * CH * n), BF16) for n in (16, 14, 12, 10)],

time: 89.2 us -> 86.5 us (0.970)
  Pallas kernels: 88.1 us -> 85.3 us
    pallas_call x1, Pallas kernels: 85.5 us -> 82.7 us  [on_device(): pl.pallas_call(functools.partial(kernel, tm_count, space_count, cols, chu...]
where the time goes in v3:
time: 86.5 us; the launch traced here: 85.9 us
  Pallas kernels  85.3 us (99%)
    pallas_call x1, Pallas kernels, on_device(): pl.pallas_call(functools.partial(kernel, tm_count, space_count, cols, chu...  82.7 us
    pallas_call x1, Pallas kernels, on_device(): pl.pallas_call(finish, out_shape=out_shape, in_specs=[vmem, vmem, vmem],...  2.55 us

profile of v3, /device:TPU:1, one launch (start us, length us, event | category | flops | bytes accessed | tf_op | source)
XLA Modules:
  0.0 85.9 jit_solution(3812000284728727936)
XLA Ops:
  0.6 82.7 %shard_map.144 = (bf16[4,3,8,768]{3,2,1,0:T(8,128)(2,1)}, f32[1,16,8,768]{3,2,1,0:T(8,128)}, f32[40,128]{1,0:T(8,128)}) custom-call(bf16[4,3,8,768]{3,2,1,0:T(8,128)(2,1)} %frames_in.1, bf16[4,16,8,768]{3,2,1,0:T(8,128)(2,1)} %states_in.1, bf16[16,8,768]{2,1,0:T(8,128)(2,1)} %start_in.1, bf16[4,12,8,768]{3,2,1,0:T(8,128)(2,1)} %cot_in.1, ...), custom_call_target="tpu_custom_call" | custom-call | tf_op jit(solution)/shard_map/pallas_call | solution.py:752
  83.4 2.6 %shard_map.145 = (f32[9,16,16]{2,1,0:T(8,128)}, f32[9,3,16]{2,1,0:T(4,128)}, f32[16]{0:T(128)}, f32[16]{0:T(128)}, f32[12,16]{1,0:T(8,128)}, /*index=5*/bf16[4,3,8,768]{3,2,1,0:T(8,128)(2,1)}, f32[1,16,8,768]{3,2,1,0:T(8,128)}) custom-call(f32[40,128]{1,0:T(8,128)} %get-tuple-element.17.sums_ref, bf16[4,3,8,768]{3,2,1,0:T(8,128)(2,1)} %get-tuple-element.18.gf_in, ...), custom_call_target="tpu_custom_call" | custom-call | tf_op jit(solution)/shard_map/pallas_call | solution.py:777

commit v4 on v3

--- a/solution.py
+++ b/solution.py
@@ -16,8 +16,9 @@
 STEPS = 4
 HALO = [STEPS + 1 - k for k in range(STEPS)]
 A_AT = [0, 5, 9]
-B_AT = [12, 17, 21, 24]
-MSG = 26 * CH
+B_AT = [12, 16, 19, 21]
+RIM_AT = 22
+MSG = 23 * CH
 TILE = ROWS * CH
 
 
@@ -52,12 +53,12 @@
 def kernel(
     tm_count, space_count, cols, chunks,
     frames_in, states_in, start_in, cot_in, wrec_ref, win_ref, bias_ref, retain_ref, whead_ref,
-    gf_ref, bound_ref, sums_ref,
-    frames_ref, states_ref, start_ref, cot_ref,
+    gf_out, bound_out, sums_ref,
+    gf_ref, bound_ref, frames_ref, states_ref, start_ref, cot_ref,
     zpa, zpb, zpq, stage_up, stage_dn, h_up, h_dn, p_up, p_dn, oldx,
     slopes, pushed, xs, dkeep, gkeep, gfs, bnd, c_own, c_up, c_dn, c_send, l_own, l_up, l_dn, l_send,
-    wf0, wf1, wf2, wf3, wp, wt0, wt1, wt2, wt3, d1prev, d2prev, gprev, biasb, retb, gram, headacc, rpart, rs, ag, red,
-    h_ssem, h_rsem, p_ssem, p_rsem, e_ssem, c_ssem, c_rsem, s1, r1, s2, r2, s3, r3, in_sem,
+    wf0, wf1, wf2, wf3, wp, wt0, wt1, wt2, wt3, wc, d1prev, d2prev, gprev, biasb, retb, gram, headacc, rpart, rs, ag, red,
+    h_ssem, h_rsem, p_ssem, p_rsem, e_ssem, c_ssem, c_rsem, s1, r1, s2, r2, s3, r3, in_sem, out_sem,
 ):
     tm = lax.axis_index("tm")
     sp = lax.axis_index("space")
@@ -220,15 +221,24 @@
 
             p_copy(j, 0).start()
 
+        rims = [[], []]
         for k in range(STEPS):
             h = HALO[k]
             b_val = zpb[STEPS - 1 - k, j + 1]
-            stage_up[j, B_AT[k] * CH : (B_AT[k] + h) * CH] = b_val[: h * CH]
-            stage_dn[j, B_AT[k] * CH : (B_AT[k] + h) * CH] = b_val[TILE - h * CH :]
+            stage_up[j, B_AT[k] * CH : (B_AT[k] + h - 1) * CH] = b_val[: (h - 1) * CH]
+            stage_dn[j, B_AT[k] * CH : (B_AT[k] + h - 1) * CH] = b_val[TILE - (h - 1) * CH :]
+            rims[0].append(b_val[(h - 1) * CH : h * CH].astype(F32))
+            rims[1].append(b_val[TILE - h * CH : TILE - (h - 1) * CH].astype(F32))
             if k < STEPS - 1:
                 a_val = zpa[STEPS - 2 - k, j + 1]
                 stage_up[j, A_AT[k] * CH : (A_AT[k] + h) * CH] = a_val[: h * CH]
                 stage_dn[j, A_AT[k] * CH : (A_AT[k] + h) * CH] = a_val[TILE - h * CH :]
+
+        for stage, rim in ((stage_up, rims[0]), (stage_dn, rims[1])):
+            value = rim[0]
+            for k in range(1, STEPS):
+                value = jnp.where(iota2((CH, 1), 0) >= 4 * k, pltpu.roll(rim[k], 4 * k, 0), value)
+            stage[j, RIM_AT * CH : (RIM_AT + 1) * CH] = value.astype(BF16)
 
         @pl.when(has_up)
         def _():
@@ -297,34 +307,39 @@
                 ahead = row_in - r
                 value = jnp.where(ahead == 0, base[0], jnp.where(ahead == 1, base[1], jnp.where(ahead == 2, base[2], 0.0)))
                 wf[k][CH * r : CH * (r + 1)] = value.astype(BF16)
-            size = CH * n
+            half = n // 2 - 1
+            size = CH * (half + 2)
             at = iota2((1, 3 * size), 1)
             part = at // size
             row_in = lax.rem(at, size) // CH
             chan = lax.rem(at, CH)
             picks = [onehot((iota2((CH, 3 * size), 0) == chan) & (part == b)) for b in range(3)]
             base = []
-            base_in = []
             for a in range(3):
                 total = jnp.zeros((CH, 3 * size), F32)
-                total_in = jnp.zeros((32, 3 * size), F32)
                 for b in range(3):
-                    t = 3 * a + b
-                    total = total + dot_tn(rec[t], picks[b])
-                    total_in = total_in + dot(inp_rows[t], picks[b])
+                    total = total + dot_tn(rec[3 * a + b], picks[b])
                 base.append(total)
-                base_in.append(total_in)
-            for r in range(n - 2):
+            for r in range(half):
                 behind = r + 2 - row_in
                 value = jnp.where(
                     behind == 0, base[0], jnp.where(behind == 1, base[1], jnp.where(behind == 2, base[2], 0.0))
                 )
                 wt[k][CH * r : CH * (r + 1)] = value.astype(BF16)
-            behind = lax.rem(iota2((32, 1), 0), ROWS) + 2 - (row_in - (STEPS - 1 - k))
-            value = jnp.where(
-                behind == 0, base_in[0], jnp.where(behind == 1, base_in[1], jnp.where(behind == 2, base_in[2], 0.0))
-            )
-            wt[k][CH * (n - 2) : CH * n] = value.astype(BF16)
+        size = 10 * CH
+        at = iota2((1, 3 * size), 1)
+        part = at // size
+        row_in = lax.rem(at, size) // CH
+        chan = lax.rem(at, CH)
+        picks = [onehot((iota2((CH, 3 * size), 0) == chan) & (part == b)) for b in range(3)]
+        behind = lax.rem(iota2((32, 1), 0), ROWS) + 2 - row_in
+        value = jnp.zeros((32, 3 * size), F32)
+        for a in range(3):
+            total = jnp.zeros((32, 3 * size), F32)
+            for b in range(3):
+                total = total + dot(inp_rows[3 * a + b], picks[b])
+            value = jnp.where(behind == a, total, value)
+        wc[...] = value.astype(BF16)
         pick = onehot(iota2((12, 256), 0) == lax.rem(iota2((12, 256), 1), CH) - 4)
         base_h = dot_tn(whead_ref[...], pick)
         for r in range(16):
@@ -360,10 +375,18 @@
                     dn_a = h_dn[slot, A_AT[k] * CH : (A_AT[k] + h) * CH]
                 else:
                     up_a, dn_a = p_up[slot], p_dn[slot]
-                up_b = h_up[slot, B_AT[k] * CH : (B_AT[k] + h) * CH]
-                dn_b = h_dn[slot, B_AT[k] * CH : (B_AT[k] + h) * CH]
+                up_b = h_up[slot, B_AT[k] * CH : (B_AT[k] + h - 1) * CH]
+                dn_b = h_dn[slot, B_AT[k] * CH : (B_AT[k] + h - 1) * CH]
+                rims = []
+                for ref in (h_up, h_dn):
+                    rim = ref[slot, RIM_AT * CH : (RIM_AT + 1) * CH]
+                    if k > 0:
+                        rim = pltpu.roll(rim.astype(F32), CH - 4 * k, 0).astype(BF16)
+                    rims.append(rim)
                 own_a = zpa[STEPS - 2 - k, slot] if k < STEPS - 1 else zpq[slot]
-                return jnp.concatenate([up_a, own_a, dn_a, up_b, zpb[STEPS - 1 - k, slot], dn_b], axis=0)
+                return jnp.concatenate(
+                    [up_a, own_a, dn_a, rims[0], up_b, zpb[STEPS - 1 - k, slot], dn_b, rims[1]], axis=0
+                )
 
             raw = whole(j + 1)
             size = CH * (n + 2)
@@ -464,10 +487,18 @@
             inner = g[CH : size - CH]
             rg, gs = shifted(inner, gprev[k, 0 : size - 2 * CH], 1)
             gprev[k, 0 : size - 2 * CH] = rg
-            conv = dot(wt[k][...], jnp.concatenate([d, d1, d2], axis=0))
-            carried = retb[0 : size - 2 * CH] * gs + conv[0 : size - 2 * CH]
-            gfs[j, k] = conv[size - 2 * CH : size]
+            taps = [d, d1, d2]
+            half = CH * (n // 2 - 1)
+            conv = jnp.concatenate(
+                [
+                    dot(wt[k][...], jnp.concatenate([t[at : at + half + 2 * CH] for t in taps], axis=0))
+                    for at in (0, half)
+                ],
+                axis=0,
+            )
+            carried = retb[0 : size - 2 * CH] * gs + conv
             at = (STEPS - k) * CH
+            gfs[j, k] = dot(wc[...], jnp.concatenate([t[at - CH : at + 9 * CH] for t in taps], axis=0))
             dkeep[j, k] = d[at : at + TILE]
             gkeep[j, k] = g[at : at + TILE].astype(BF16)
         out = carried.astype(BF16)
@@ -555,6 +586,11 @@
 
     out_shift = skew0 + STEPS + 1
 
+    moves = [
+        pltpu.make_async_copy(gf_ref, gf_out, out_sem.at[0]),
+        pltpu.make_async_copy(bound_ref, bound_out, out_sem.at[1]),
+    ]
+
     def put_outputs():
         for c in range(blocks):
             def unskew(now, after, shift):
@@ -566,6 +602,8 @@
             for k in range(STEPS):
                 value = unskew(gfs[c, k, 0:24], gfs[c + 1, k, 0:24], skew0 + k + 2)
                 gf_ref[STEPS - 1 - k, :, :, W * c : W * (c + 1)] = value.reshape(3, ROWS, W).astype(BF16)
+        for move in moves:
+            move.start()
 
     def second_copy(q):
         s = lax.rem(sp + q, space_count)
@@ -605,6 +643,8 @@
         third_copy(1).wait_recv()
 
     sums_ref[...] = red[...]
+    for move in moves:
+        move.wait()
 
     @pl.when(is_first)
     def _():
@@ -702,6 +742,8 @@
     anywhere = pl.BlockSpec(memory_space=pl.ANY)
     dma = pltpu.SemaphoreType.DMA
     scratch = [
+        pltpu.VMEM(frames.shape, BF16),
+        pltpu.VMEM((1, CH, ROWS, cols), F32),
         pltpu.VMEM(frames.shape, BF16),
         pltpu.VMEM(states.shape, BF16),
         pltpu.VMEM(start_state.shape, BF16),
@@ -730,7 +772,8 @@
         *[pltpu.VMEM((2 * CH, W), BF16)] * 4,
         *[pltpu.VMEM((CH * n, 6 * CH * (n + 2)), BF16) for n in (16, 14, 12, 10)],
         pltpu.VMEM((256, 256), BF16),
-        *[pltpu.VMEM((CH * n, 3 * CH * n), BF16) for n in (16, 14, 12, 10)],
+        *[pltpu.VMEM((CH * h, 3 * CH * (h + 2)), BF16) for h in (7, 6, 5, 4)],
+        pltpu.VMEM((32, 30 * CH), BF16),
         pltpu.VMEM((STEPS, 256, W), BF16),
         pltpu.VMEM((STEPS, 256, W), BF16),
         pltpu.VMEM((STEPS, 256, W), F32),
@@ -747,7 +790,7 @@
         dma((3, chunks)), dma((3, chunks)),
         dma((tm_count,)), dma((tm_count,)),
         dma((space_count,)), dma((space_count,)),
-        dma((tm_count,)), dma((tm_count,)), dma((4,)),
+        dma((tm_count,)), dma((tm_count,)), dma((4,)), dma((2,)),
     ]
     grad_frames, bound, sums = pl.pallas_call(
         functools.partial(kernel, tm_count, space_count, cols, chunks),
@@ -757,7 +800,7 @@
             jax.ShapeDtypeStruct((40, W), F32),
         ],
         in_specs=[anywhere] * 4 + [vmem] * 5,
-        out_specs=[vmem] * 3,
+        out_specs=[anywhere, anywhere, vmem],
         scratch_shapes=scratch,
         compiler_params=pltpu.CompilerParams(
             collective_id=0, has_side_effects=True, vmem_limit_bytes=56 * 1024 * 1024

time: 86.5 us -> 84.1 us (0.972)
  Pallas kernels: 85.3 us -> 82.9 us
    pallas_call x1, Pallas kernels: 82.7 us -> 80.4 us  [on_device(): pl.pallas_call(functools.partial(kernel, tm_count, space_count, cols, chu...]
where the time goes in v4:
time: 84.1 us; the launch traced here: 83.6 us
  Pallas kernels  82.9 us (99%)
    pallas_call x1, Pallas kernels, on_device(): pl.pallas_call(functools.partial(kernel, tm_count, space_count, cols, chu...  80.4 us
    pallas_call x1, Pallas kernels, on_device(): pl.pallas_call(finish, out_shape=out_shape, in_specs=[vmem, vmem, vmem],...  2.55 us

profile of v4, /device:TPU:1, one launch (start us, length us, event | category | flops | bytes accessed | tf_op | source)
XLA Modules:
  0.0 83.6 jit_solution(11133846579632804070)
XLA Ops:
  0.6 80.4 %shard_map.144 = (bf16[4,3,8,768]{3,2,1,0:T(8,128)(2,1)}, f32[1,16,8,768]{3,2,1,0:T(8,128)}, f32[40,128]{1,0:T(8,128)}) custom-call(bf16[4,3,8,768]{3,2,1,0:T(8,128)(2,1)} %frames_in.1, bf16[4,16,8,768]{3,2,1,0:T(8,128)(2,1)} %states_in.1, bf16[16,8,768]{2,1,0:T(8,128)(2,1)} %start_in.1, bf16[4,12,8,768]{3,2,1,0:T(8,128)(2,1)} %cot_in.1, ...), custom_call_target="tpu_custom_call" | custom-call | tf_op jit(solution)/shard_map/pallas_call | solution.py:795
  81.0 2.6 %shard_map.145 = (f32[9,16,16]{2,1,0:T(8,128)}, f32[9,3,16]{2,1,0:T(4,128)}, f32[16]{0:T(128)}, f32[16]{0:T(128)}, f32[12,16]{1,0:T(8,128)}, /*index=5*/bf16[4,3,8,768]{3,2,1,0:T(8,128)(2,1)}, f32[1,16,8,768]{3,2,1,0:T(8,128)}) custom-call(f32[40,128]{1,0:T(8,128)} %get-tuple-element.17.sums_ref, bf16[4,3,8,768]{3,2,1,0:T(8,128)(2,1)} %get-tuple-element.18.gf_in, ...), custom_call_target="tpu_custom_call" | custom-call | tf_op jit(solution)/shard_map/pallas_call | solution.py:820

commit v5 on v4

--- a/solution.py
+++ b/solution.py
@@ -84,6 +84,50 @@
     zh = jnp.zeros((MSG, W), BF16)
     z2 = jnp.zeros((2 * CH, W), BF16)
     zt = jnp.zeros((TILE, W), BF16)
+    @pl.when(jnp.logical_not(has_up))
+    def _():
+        for j in range(blocks):
+            h_up[j + 1] = zh
+            p_up[j + 1] = z2
+        for j in range(chunks):
+            c_up[j] = jnp.zeros((STEPS * CH, W), BF16)
+
+    @pl.when(jnp.logical_not(has_dn))
+    def _():
+        for j in range(blocks):
+            h_dn[j + 1] = zh
+            p_dn[j + 1] = z2
+        for j in range(chunks):
+            c_dn[j] = jnp.zeros((STEPS * CH, W), BF16)
+
+    @pl.when(is_last)
+    def _():
+        for j in range(chunks):
+            c_own[j] = jnp.zeros((TILE, W), BF16)
+            c_up[j] = jnp.zeros((STEPS * CH, W), BF16)
+            c_dn[j] = jnp.zeros((STEPS * CH, W), BF16)
+
+    barrier = pltpu.get_barrier_semaphore()
+
+    def greet(t, s):
+        pl.semaphore_signal(barrier, inc=1, device_id=(t, s), device_id_type=MESH)
+
+    for dt in (0, 1, tm_count - 1):
+        for ds in (0, 1, space_count - 1):
+            if dt or ds:
+                greet(lax.rem(tm + dt, tm_count), lax.rem(sp + ds, space_count))
+
+    @pl.when(jnp.logical_not(is_first))
+    def _():
+        greet(0, sp)
+
+    @pl.when(is_first)
+    def _():
+        for t in range(1, tm_count):
+            greet(t, sp)
+        for q in range(1, space_count):
+            greet(0, lax.rem(sp + q, space_count))
+
     for slot in [0] + list(range(blocks + 1, chunks + 1)):
         h_up[slot] = zh
         h_dn[slot] = zh
@@ -101,47 +145,6 @@
         d2prev[k] = jnp.zeros((16 * CH, W), BF16)
     gram[...] = jnp.zeros_like(gram)
 
-    @pl.when(jnp.logical_not(has_up))
-    def _():
-        for j in range(blocks):
-            h_up[j + 1] = zh
-            p_up[j + 1] = z2
-        l_up[...] = z2
-        for j in range(blocks):
-            c_up[j] = jnp.zeros((STEPS * CH, W), BF16)
-
-    @pl.when(jnp.logical_not(has_dn))
-    def _():
-        for j in range(blocks):
-            h_dn[j + 1] = zh
-            p_dn[j + 1] = z2
-        l_dn[...] = z2
-        for j in range(blocks):
-            c_dn[j] = jnp.zeros((STEPS * CH, W), BF16)
-
-    @pl.when(is_last)
-    def _():
-        l_own[...] = z2
-        l_up[...] = z2
-        l_dn[...] = z2
-        for j in range(blocks):
-            c_own[j] = jnp.zeros((TILE, W), BF16)
-            c_up[j] = jnp.zeros((STEPS * CH, W), BF16)
-            c_dn[j] = jnp.zeros((STEPS * CH, W), BF16)
-
-    barrier = pltpu.get_barrier_semaphore()
-
-    def greet(t, s):
-        pl.semaphore_signal(barrier, inc=1, device_id=(t, s), device_id_type=MESH)
-
-    for p in range(1, tm_count):
-        greet(lax.rem(tm + p, tm_count), sp)
-    for q in range(1, space_count):
-        greet(tm, lax.rem(sp + q, space_count))
-    for dt in (1, tm_count - 1):
-        for ds in (1, space_count - 1):
-            greet(lax.rem(tm + dt, tm_count), lax.rem(sp + ds, space_count))
-
     pr = iota2((TILE, TILE), 0)
     pc = iota2((TILE, TILE), 1)
     perm_a = onehot((pr // CH == lax.rem(pc, ROWS)) & (lax.rem(pr, CH) == pc // ROWS))
@@ -171,7 +174,7 @@
     def _():
         put(zpq, dot(perm_a, flat(start_ref[...], CH).astype(BF16)))
 
-    pl.semaphore_wait(barrier, tm_count - 1 + space_count - 1 + 4)
+    pl.semaphore_wait(barrier, 8 + jnp.where(is_first, tm_count - 1 + space_count - 1, 1))
 
     def h_copy(j, up):
         src, dst, target = (stage_up, h_dn, sp - 1) if up else (stage_dn, h_up, sp + 1)
@@ -465,16 +468,14 @@
     group = 2 * CH
     spread_w = W // 4
 
-    def unpack(ref, which):
+    def unpack(ref, dst, which):
         value = ref[...]
-        return [value if q == 0 else pltpu.roll(value, W - spread_w * q, 1) for q in which]
-
-    def chain(j, last):
-        if last:
-            parts = unpack(l_up, (2, 3)) + unpack(l_own, (0, 1, 2, 3)) + unpack(l_dn, (0, 1))
-        else:
-            parts = [c_up[j], c_own[j], c_dn[j]]
-        carried = jnp.concatenate(parts, axis=0).astype(F32)
+        for at, q in enumerate(which):
+            part = value if q == 0 else pltpu.roll(value, W - spread_w * q, 1)
+            dst[blocks, group * at : group * (at + 1)] = part
+
+    def chain(j):
+        carried = jnp.concatenate([c_up[j], c_own[j], c_dn[j]], axis=0).astype(F32)
         for k in range(STEPS):
             n = 16 - 2 * k
             size = CH * n
@@ -501,50 +502,67 @@
             gfs[j, k] = dot(wc[...], jnp.concatenate([t[at - CH : at + 9 * CH] for t in taps], axis=0))
             dkeep[j, k] = d[at : at + TILE]
             gkeep[j, k] = g[at : at + TILE].astype(BF16)
-        out = carried.astype(BF16)
-        if last:
-            packed = out[0:group]
+        c_send[j] = carried.astype(BF16)
+        bnd[j] = carried
+
+    def await_carried(hop):
+        hop(0).wait_recv()
+
+        @pl.when(has_dn)
+        def _():
+            hop(1).wait_recv()
+
+        @pl.when(has_up)
+        def _():
+            hop(2).wait_recv()
+
+    def start_carried(hop):
+        @pl.when(has_up)
+        def _():
+            hop(1).start()
+
+        @pl.when(has_dn)
+        def _():
+            hop(2).start()
+
+        hop(0).start()
+
+    def step(j, carry):
+        @pl.when(is_last)
+        def _():
+            prepare(j, 0)
+
+        @pl.when(jnp.logical_not(is_last) & (j < blocks))
+        def _():
+            await_carried(functools.partial(c_copy, j))
+
+        @pl.when(jnp.logical_not(is_last) & (j == blocks))
+        def _():
+            await_carried(l_copy)
+            unpack(l_own, c_own, (0, 1, 2, 3))
+
+            @pl.when(has_up)
+            def _():
+                unpack(l_up, c_up, (2, 3))
+
+            @pl.when(has_dn)
+            def _():
+                unpack(l_dn, c_dn, (0, 1))
+
+        chain(j)
+
+        @pl.when(jnp.logical_not(is_first) & (j < blocks))
+        def _():
+            start_carried(functools.partial(c_copy, j))
+
+        @pl.when(jnp.logical_not(is_first) & (j == blocks))
+        def _():
+            packed = c_send[blocks, 0:group]
             for q in range(1, 4):
-                packed = jnp.where(
-                    lane >= spread_w * q, pltpu.roll(out[group * q : group * (q + 1)], spread_w * q, 1), packed
-                )
+                turned = pltpu.roll(c_send[blocks, group * q : group * (q + 1)], spread_w * q, 1)
+                packed = jnp.where(lane >= spread_w * q, turned, packed)
             l_send[...] = packed
-        else:
-            c_send[j] = out
-        bnd[j] = carried
-
-    def step(j, carry, last=False):
-        hop = l_copy if last else functools.partial(c_copy, j)
-
-        @pl.when(is_early)
-        def _():
-            prepare(j, 0)
-
-        @pl.when(jnp.logical_not(is_last))
-        def _():
-            hop(0).wait_recv()
-
-            @pl.when(has_dn)
-            def _():
-                hop(1).wait_recv()
-
-            @pl.when(has_up)
-            def _():
-                hop(2).wait_recv()
-
-        chain(j, last)
-
-        @pl.when(jnp.logical_not(is_first))
-        def _():
-            @pl.when(has_up)
-            def _():
-                hop(1).start()
-
-            @pl.when(has_dn)
-            def _():
-                hop(2).start()
-
-            hop(0).start()
+            start_carried(l_copy)
 
         @pl.when(jnp.logical_not(is_early))
         def _():
@@ -557,8 +575,7 @@
         head_gradient()
         lax.fori_loop(0, chunks, prepare, 0)
 
-    lax.fori_loop(0, blocks, step, 0)
-    step(blocks, 0, True)
+    lax.fori_loop(0, chunks, step, 0)
 
     @pl.when(is_early)
     def _():
@@ -765,10 +782,10 @@
         pltpu.VMEM((chunks, STEPS, TILE, W), BF16),
         pltpu.VMEM((chunks, STEPS, 32, W), F32),
         pltpu.VMEM((chunks, TILE, W), F32),
-        pltpu.VMEM((blocks, TILE, W), BF16),
-        pltpu.VMEM((blocks, STEPS * CH, W), BF16),
-        pltpu.VMEM((blocks, STEPS * CH, W), BF16),
-        pltpu.VMEM((blocks, TILE, W), BF16),
+        pltpu.VMEM((chunks, TILE, W), BF16),
+        pltpu.VMEM((chunks, STEPS * CH, W), BF16),
+        pltpu.VMEM((chunks, STEPS * CH, W), BF16),
+        pltpu.VMEM((chunks, TILE, W), BF16),
         *[pltpu.VMEM((2 * CH, W), BF16)] * 4,
         *[pltpu.VMEM((CH * n, 6 * CH * (n + 2)), BF16) for n in (16, 14, 12, 10)],
         pltpu.VMEM((256, 256), BF16),

time: 84.1 us -> 83.6 us (level)
  no operation moved by 1% of the time
where the time goes in v5:
time: 83.6 us; the launch traced here: 83.1 us
  Pallas kernels  82.5 us (99%)
    pallas_call x1, Pallas kernels, on_device(): pl.pallas_call(functools.partial(kernel, tm_count, space_count, cols, chu...  79.9 us
    pallas_call x1, Pallas kernels, on_device(): pl.pallas_call(finish, out_shape=out_shape, in_specs=[vmem, vmem, vmem],...  2.55 us

profile of v5, /device:TPU:1, one launch (start us, length us, event | category | flops | bytes accessed | tf_op | source)
XLA Modules:
  0.0 83.1 jit_solution(15124027861226453793)
XLA Ops:
  0.6 79.9 %shard_map.144 = (bf16[4,3,8,768]{3,2,1,0:T(8,128)(2,1)}, f32[1,16,8,768]{3,2,1,0:T(8,128)}, f32[40,128]{1,0:T(8,128)}) custom-call(bf16[4,3,8,768]{3,2,1,0:T(8,128)(2,1)} %frames_in.1, bf16[4,16,8,768]{3,2,1,0:T(8,128)(2,1)} %states_in.1, bf16[16,8,768]{2,1,0:T(8,128)(2,1)} %start_in.1, bf16[4,12,8,768]{3,2,1,0:T(8,128)(2,1)} %cot_in.1, ...), custom_call_target="tpu_custom_call" | custom-call | tf_op jit(solution)/shard_map/pallas_call | solution.py:812
  80.6 2.6 %shard_map.145 = (f32[9,16,16]{2,1,0:T(8,128)}, f32[9,3,16]{2,1,0:T(4,128)}, f32[16]{0:T(128)}, f32[16]{0:T(128)}, f32[12,16]{1,0:T(8,128)}, /*index=5*/bf16[4,3,8,768]{3,2,1,0:T(8,128)(2,1)}, f32[1,16,8,768]{3,2,1,0:T(8,128)}) custom-call(f32[40,128]{1,0:T(8,128)} %get-tuple-element.17.sums_ref, bf16[4,3,8,768]{3,2,1,0:T(8,128)(2,1)} %get-tuple-element.18.gf_in, ...), custom_call_target="tpu_custom_call" | custom-call | tf_op jit(solution)/shard_map/pallas_call | solution.py:837

commit v6 on v5

--- a/solution.py
+++ b/solution.py
@@ -66,7 +66,7 @@
     has_dn = sp < space_count - 1
     is_last = tm == tm_count - 1
     is_first = tm == 0
-    is_early = tm >= tm_count - 1
+    is_early = tm >= tm_count - 2
     blocks = cols // W
     wf = [wf0, wf1, wf2, wf3]
     wt = [wt0, wt1, wt2, wt3]
@@ -573,6 +573,9 @@
     @pl.when(jnp.logical_not(is_early))
     def _():
         head_gradient()
+
+    @pl.when(jnp.logical_not(is_last))
+    def _():
         lax.fori_loop(0, chunks, prepare, 0)
 
     lax.fori_loop(0, chunks, step, 0)

time: 83.6 us -> 83.6 us (level)
  no operation moved by 1% of the time
where the time goes in v6:
time: 83.6 us; the launch traced here: 83.1 us
  Pallas kernels  82.5 us (99%)
    pallas_call x1, Pallas kernels, on_device(): pl.pallas_call(functools.partial(kernel, tm_count, space_count, cols, chu...  79.9 us
    pallas_call x1, Pallas kernels, on_device(): pl.pallas_call(finish, out_shape=out_shape, in_specs=[vmem, vmem, vmem],...  2.55 us

profile of v6, /device:TPU:1, one launch (start us, length us, event | category | flops | bytes accessed | tf_op | source)
XLA Modules:
  0.0 83.1 jit_solution(18053876111106953837)
XLA Ops:
  0.6 79.9 %shard_map.144 = (bf16[4,3,8,768]{3,2,1,0:T(8,128)(2,1)}, f32[1,16,8,768]{3,2,1,0:T(8,128)}, f32[40,128]{1,0:T(8,128)}) custom-call(bf16[4,3,8,768]{3,2,1,0:T(8,128)(2,1)} %frames_in.1, bf16[4,16,8,768]{3,2,1,0:T(8,128)(2,1)} %states_in.1, bf16[16,8,768]{2,1,0:T(8,128)(2,1)} %start_in.1, bf16[4,12,8,768]{3,2,1,0:T(8,128)(2,1)} %cot_in.1, ...), custom_call_target="tpu_custom_call" | custom-call | tf_op jit(solution)/shard_map/pallas_call | solution.py:815
  80.6 2.6 %shard_map.145 = (f32[9,16,16]{2,1,0:T(8,128)}, f32[9,3,16]{2,1,0:T(4,128)}, f32[16]{0:T(128)}, f32[16]{0:T(128)}, f32[12,16]{1,0:T(8,128)}, /*index=5*/bf16[4,3,8,768]{3,2,1,0:T(8,128)(2,1)}, f32[1,16,8,768]{3,2,1,0:T(8,128)}) custom-call(f32[40,128]{1,0:T(8,128)} %get-tuple-element.17.sums_ref, bf16[4,3,8,768]{3,2,1,0:T(8,128)(2,1)} %get-tuple-element.18.gf_in, ...), custom_call_target="tpu_custom_call" | custom-call | tf_op jit(solution)/shard_map/pallas_call | solution.py:840
